TPU v7x, 256 devices: a whole 4x4x8 slice. The times are simulated.
256 devices in a mesh: gz: 8 (over y, core), gx: 8 (over x, z_lo), gy: 4 (over z_hi).
Axes of the slice: x: 4, y: 4, z: 8 (z_hi: 4, z_lo: 2; z = z_hi * 2 + z_lo), core: 2. Of those that a mesh axis runs over, the one named last changes fastest.
Arguments:
- initial_field: float32 [16, 1024, 512], P('gz', 'gx', 'gy'), may hold values from -6 to 6
- source_term: float32 [16, 1024, 512], P('gz', 'gx', 'gy'), may hold values from -48 to 48
- block_inverse: float32 [1024, 512, 128], P('gx', 'gy'), may hold values from -0.1 to 0.1
Outputs:
- smoothed: float32 [16, 1024, 512], P('gz', 'gx', 'gy')
All inputs are finite; a program needn't handle non-finite values.
Results may differ from a plain program's by a relative error of at most 0.00013.
Values sent between devices are 32-bit elements; how exact they have to be, the bound alone decides.
A program may use at most 64 MiB of HBM per device.

v0:
```python
import jax
import jax.numpy as jnp
from jax import lax
from jax.sharding import PartitionSpec as P

exact_mode = lax.Precision.HIGHEST


def extended_2(cells, sides, width):
    for axis, dim in sides:
        count = lax.axis_size(axis)
        ends = count - 1
        head = lax.slice_in_dim(cells, 0, width, axis=dim)
        tail = lax.slice_in_dim(cells, cells.shape[dim] - width, cells.shape[dim], axis=dim)
        cells = jnp.concatenate(
            [
                lax.ppermute(tail, axis, [(i, (i + 1) % count) for i in range(ends)]),
                cells,
                lax.ppermute(head, axis, [((i + 1) % count, i) for i in range(ends)]),
            ],
            axis=dim,
        )
    return cells


def passed_along(value, axis, steps):
    count = lax.axis_size(axis)
    first, last = (max(0, -steps), min(count, count - steps))
    return lax.ppermute(value, axis, [(source, source + steps) for source in range(first, last)])


def box_sum(extended):
    row_sums = extended[:-2] + extended[1:-1] + extended[2:]
    return row_sums[:, :-2] + row_sums[:, 1:-1] + row_sums[:, 2:]


def relax_plane(under_ext, current, over_ext, source_plane, inverse_rows):
    neighbours = box_sum(under_ext) + box_sum(current) + box_sum(over_ext)
    interior = current[1:-1, 1:-1]
    residual = source_plane - (27.0 * interior - neighbours)
    return interior + jnp.einsum("xij,xj->xi", inverse_rows, residual, precision=exact_mode)


def add_rim(plane):
    return extended_2(plane, (("gx", 0), ("gy", 1)), 1)


def run_chain(initial_field, source_term, block_inverse):
    planes_dev = initial_field.shape[0]
    chain_len = lax.axis_size("gz")
    position = lax.axis_index("gz")

    def relax_here(under_ext, current, over_ext, source_plane):
        return relax_plane(under_ext, current, over_ext, source_plane, block_inverse)

    def keep_plane(under_ext, current, over_ext, source_plane):
        return current[1:-1, 1:-1]

    old_ext = extended_2(initial_field, (("gx", 1), ("gy", 2)), 1)
    over_slab = passed_along(old_ext[0], "gz", -1)
    zero_ext = jnp.zeros_like(old_ext[0])

    def forward_section(section_num, state_now):
        fwd_ext, below_keep = state_now
        active = section_num == position
        incoming = passed_along(fwd_ext[planes_dev - 1, 1:-1, 1:-1], "gz", 1)
        under_ext = add_rim(incoming)
        below_keep = jnp.where(active, under_ext, below_keep)
        planes = []
        lower_ext = under_ext
        for j in range(planes_dev):
            upper_ext = fwd_ext[j + 1] if j + 1 < planes_dev else over_slab
            fresh = lax.cond(
                active, relax_here, keep_plane, lower_ext, fwd_ext[j], upper_ext, source_term[j]
            )
            fresh_ext = jnp.where(active, add_rim(fresh), fwd_ext[j])
            planes.append(fresh_ext)
            lower_ext = fresh_ext
        return (jnp.stack(planes), below_keep)

    fwd_ext, below_keep = lax.fori_loop(0, chain_len, forward_section, (old_ext, zero_ext))

    def backward_section(section_num, bwd_ext):
        active = section_num == chain_len - 1 - position
        incoming = passed_along(bwd_ext[0, 1:-1, 1:-1], "gz", -1)
        over_ext = add_rim(incoming)
        planes = [None] * planes_dev
        upper_ext = over_ext
        for j in reversed(range(planes_dev)):
            lower_ext = fwd_ext[j - 1] if j > 0 else below_keep
            fresh = lax.cond(
                active, relax_here, keep_plane, lower_ext, bwd_ext[j], upper_ext, source_term[j]
            )
            if j > 0:
                fresh_ext = jnp.where(active, add_rim(fresh), bwd_ext[j])
            else:
                fresh_ext = jnp.where(active, jnp.pad(fresh, 1), bwd_ext[j])
            planes[j] = fresh_ext
            upper_ext = fresh_ext
        return jnp.stack(planes)

    bwd_ext = lax.fori_loop(0, chain_len, backward_section, fwd_ext)
    return bwd_ext[:, 1:-1, 1:-1]


def body(initial_field, source_term, block_inverse):
    return run_chain(initial_field, source_term, block_inverse)


def solution(mesh):
    placed = (P("gz", "gx", "gy"), P("gz", "gx", "gy"), P("gx", "gy", None))
    return jax.shard_map(
        body, mesh=mesh, in_specs=placed, out_specs=P("gz", "gx", "gy"), check_vma=False
    )
```

profile of v0, /device:TPU:166, one launch (start us, length us, event | category | flops | bytes accessed | tf_op | source)
XLA Modules:
  0.0 1349.2 jit_solution(11736237281752747053)
XLA Ops:
  25.7 613.4 %while.32 = (s32[]{:T(128)}, f32[2,130,130]{2,1,0:T(8,128)S(1)}, f32[130,130]{1,0:T(8,128)S(1)}, s32[]{:T(128)}, f32[2,128,128]{2,1,0:T(8,128)}, /*index=5*/f32[...) while((s32[]{:T(128)}, f32[2,130,130]{2,1,0:T(8,128)S(1)}, ...), condition=%wide.region_5.6_spmd.clone, body=%wide.region_0.5_spmd.clone.sunk | while | flops 51345488 | bytes 23155080 | solution.py:81
  25.8 5.0 collective-permute-start.9
  41.4 5.5 collective-permute-start.12
  49.3 6.7 collective-permute-done.13
  56.1 16.6 %conditional.12 = (f32[128,128]{1,0:T(8,128)S(1)}) conditional(s32[]{:T(128)} %convert_element_type.31, f32[130,130]{1,0:T(8,128)S(1)} %get-tuple-element.664, (f32[130,130]{1,0:T(8,128)S(1)}, f32[2,128,128]{2,1,0:T(8,128)}, f32[130,130]{1,0:T(8,128)S(1)}, f32[130,130]{1,0:T(8,128)S(1)}, f32[128,128,128]{2,1,0:T(8,128)}) %tuple.176), branch_computations={%region_1.1_spmd, %region_2.2_spmd} | conditional | flops 25462272 | bytes 10301448 | solution.py:73
  57.3 15.4 %fusion.31 = f32[128,1,128]{2,1,0:T(1,128)S(1)} fusion(f32[128,128,1]{1,2,0:T(1,128)S(1)} %bitcast.104, f32[128,128,128]{2,1,0:T(8,128)} %get-tuple-element.392), kind=kOutput, calls=%fused_computation.98 | convolution fusion | flops 25165824 | bytes 8519680 | tf_op jit(solution)/shard_map/while/body/eval_jaxpr/cond/branch_1_fun/xij,xj->xi/dot_general | solution.py:41
  92.9 16.7 %conditional.13 = (f32[128,128]{1,0:T(8,128)S(1)}) conditional(s32[]{:T(128)} %convert_element_type.31, f32[130,130]{1,0:T(8,128)S(1)} %get-tuple-element.670, (f32[130,130]{1,0:T(8,128)S(1)}, f32[2,128,128]{2,1,0:T(8,128)}, pred[130,130]{1,0:T(8,128)(4,1)S(1)}, f32[130,130]{1,0:T(8,128)S(1)}, f32[130,130]{1,0:T(8,128)S(1)}, ...), branch_computations={%region_3.3_spmd, %region_4.4_spmd} | conditional | flops 25479172 | bytes 10521148 | solution.py:73
  94.0 15.4 %fusion.32 = f32[128,1,128]{2,1,0:T(1,128)S(1)} fusion(f32[128,128,1]{1,2,0:T(1,128)S(1)} %bitcast.105, f32[128,128,128]{2,1,0:T(8,128)} %get-tuple-element.399), kind=kOutput, calls=%fused_computation.99 | convolution fusion | flops 25165824 | bytes 8519680 | tf_op jit(solution)/shard_map/while/body/eval_jaxpr/cond/branch_1_fun/xij,xj->xi/dot_general | solution.py:41
  142.3 4.8 collective-permute-start.13
  181.2 4.8 collective-permute-start.21
  189.9 27.6 %collective-permute-start.9 = (f32[128,128]{1,0:T(8,128)S(1)}, f32[128,128]{1,0:T(8,128)S(1)}, u32[]{:S(2)}, u32[]{:S(2)}) collective-permute-start(f32[128,128]{1,0:T(8,128)S(1)} %slice_bitcast_fusion.16), channel_id=1, source_target_pairs={{0,32},{32,64},{64,96},{96,128},{128,160},{160,192},{192,224},{1,3... | collective-permute-start | bytes 196616 | tf_op jit(solution)/shard_map/while/body/eval_jaxpr/ppermute | solution.py:29
  250.0 4.8 collective-permute-start.17
  330.2 4.8 collective-permute-start.21
  338.9 31.1 %collective-permute-start.9 = (f32[128,128]{1,0:T(8,128)S(1)}, f32[128,128]{1,0:T(8,128)S(1)}, u32[]{:S(2)}, u32[]{:S(2)}) collective-permute-start(f32[128,128]{1,0:T(8,128)S(1)} %slice_bitcast_fusion.16), channel_id=1, source_target_pairs={{0,32},{32,64},{64,96},{96,128},{128,160},{160,192},{192,224},{1,3... | collective-permute-start | bytes 196616 | tf_op jit(solution)/shard_map/while/body/eval_jaxpr/ppermute | solution.py:29
  381.9 4.8 collective-permute-start.13
  401.4 4.8 collective-permute-start.17
  445.4 4.8 collective-permute-start.13
  493.3 25.0 %collective-permute-start.9 = (f32[128,128]{1,0:T(8,128)S(1)}, f32[128,128]{1,0:T(8,128)S(1)}, u32[]{:S(2)}, u32[]{:S(2)}) collective-permute-start(f32[128,128]{1,0:T(8,128)S(1)} %slice_bitcast_fusion.16), channel_id=1, source_target_pairs={{0,32},{32,64},{64,96},{96,128},{128,160},{160,192},{192,224},{1,3... | collective-permute-start | bytes 196616 | tf_op jit(solution)/shard_map/while/body/eval_jaxpr/ppermute | solution.py:29
  548.0 4.8 collective-permute-start.17
  639.2 709.2 %while.31 = (s32[]{:T(128)}, f32[2,130,130]{2,1,0:T(8,128)S(1)}, s32[]{:T(128)}, f32[2,128,128]{2,1,0:T(8,128)}, f32[2,130,130]{2,1,0:T(8,128)S(1)}, /*index=5*/...) while((s32[]{:T(128)}, f32[2,130,130]{2,1,0:T(8,128)S(1)}, s32[]{:T(128)}, ...), condition=%wide.region_11.12_spmd, body=%wide.region_6.11_spmd.sunk | while | flops 51244608 | bytes 22940776 | solution.py:102
  640.8 27.1 %collective-permute-done = f32[128,128]{1,0:T(8,128)S(1)} collective-permute-done((f32[128,128]{1,0:T(8,128)S(1)}, f32[128,128]{1,0:T(8,128)S(1)}, u32[]{:S(2)}, u32[]{:S(2)}) %collective-permute-start) | collective-permute-done | bytes 65568 | tf_op jit(solution)/shard_map/while/body/eval_jaxpr/ppermute | solution.py:29
  708.0 7.5 collective-permute-done
  755.3 24.5 %collective-permute-done = f32[128,128]{1,0:T(8,128)S(1)} collective-permute-done((f32[128,128]{1,0:T(8,128)S(1)}, f32[128,128]{1,0:T(8,128)S(1)}, u32[]{:S(2)}, u32[]{:S(2)}) %collective-permute-start) | collective-permute-done | bytes 65568 | tf_op jit(solution)/shard_map/while/body/eval_jaxpr/ppermute | solution.py:29
  819.7 7.1 collective-permute-done
  866.7 27.2 %collective-permute-done = f32[128,128]{1,0:T(8,128)S(1)} collective-permute-done((f32[128,128]{1,0:T(8,128)S(1)}, f32[128,128]{1,0:T(8,128)S(1)}, u32[]{:S(2)}, u32[]{:S(2)}) %collective-permute-start) | collective-permute-done | bytes 65568 | tf_op jit(solution)/shard_map/while/body/eval_jaxpr/ppermute | solution.py:29
  934.2 7.6 collective-permute-done
  981.6 24.1 %collective-permute-done = f32[128,128]{1,0:T(8,128)S(1)} collective-permute-done((f32[128,128]{1,0:T(8,128)S(1)}, f32[128,128]{1,0:T(8,128)S(1)}, u32[]{:S(2)}, u32[]{:S(2)}) %collective-permute-start) | collective-permute-done | bytes 65568 | tf_op jit(solution)/shard_map/while/body/eval_jaxpr/ppermute | solution.py:29
  1045.6 229.9 %collective-permute-done = f32[128,128]{1,0:T(8,128)S(1)} collective-permute-done((f32[128,128]{1,0:T(8,128)S(1)}, f32[128,128]{1,0:T(8,128)S(1)}, u32[]{:S(2)}, u32[]{:S(2)}) %collective-permute-start) | collective-permute-done | bytes 65568 | tf_op jit(solution)/shard_map/while/body/eval_jaxpr/ppermute | solution.py:29
  1294.2 16.6 %conditional.10 = (f32[128,128]{1,0:T(8,128)S(1)}) conditional(s32[]{:T(128)} %convert_element_type.30, f32[130,130]{1,0:T(8,128)S(1)} %slice_bitcast_fusion.12, (f32[130,130]{1,0:T(8,128)S(1)}, f32[2,128,128]{2,1,0:T(8,128)}, f32[2,130,130]{2,1,0:T(8,128)S(1)}, f32[130,130]{1,0:T(8,128)S(1)}, f32[128,128,128]{2,1,0:T(8,128)}) %tuple.162), branch_computations={%region_7.7_spmd, %region_8.8_spmd} | conditional | flops 25462272 | bytes 10301448 | solution.py:91
  1295.4 15.4 %fusion.33 = f32[128,1,128]{2,1,0:T(1,128)S(1)} fusion(f32[128,128,1]{1,2,0:T(1,128)S(1)} %bitcast.106, f32[128,128,128]{2,1,0:T(8,128)} %get-tuple-element.412), kind=kOutput, calls=%fused_computation.100 | convolution fusion | flops 25165824 | bytes 8519680 | tf_op jit(solution)/shard_map/while/body/eval_jaxpr/cond/branch_1_fun/xij,xj->xi/dot_general | solution.py:41
  1331.6 16.8 %conditional.11 = (f32[130,130]{1,0:T(8,128)S(1)}) conditional(s32[]{:T(128)} %convert_element_type.30, f32[130,130]{1,0:T(8,128)S(1)} %get-tuple-element.656, (f32[130,130]{1,0:T(8,128)S(1)}, f32[2,128,128]{2,1,0:T(8,128)}, f32[130,130]{1,0:T(8,128)S(1)}, pred[130,130]{1,0:T(8,128)(4,1)S(1)}, f32[130,130]{1,0:T(8,128)S(1)}, ...), branch_computations={%region_9.9_spmd, %region_10.10_spmd} | conditional | flops 25479172 | bytes 10654288 | solution.py:91
  1332.8 15.4 %fusion.34 = f32[128,1,128]{2,1,0:T(1,128)S(1)} fusion(f32[128,128,1]{1,2,0:T(1,128)S(1)} %bitcast.107, f32[128,128,128]{2,1,0:T(8,128)} %get-tuple-element.419), kind=kOutput, calls=%fused_computation.101 | convolution fusion | flops 25165824 | bytes 8519680 | tf_op jit(solution)/shard_map/while/body/eval_jaxpr/cond/branch_1_fun/xij,xj->xi/dot_general | solution.py:41
  (670 shorter events, 792.1 us)
Async XLA Ops:
  8.9 11.6 collective-permute-start.24
  12.3 9.1 collective-permute-start.25
  46.9 9.1 collective-permute-start.13
  189.9 28.5 %collective-permute-start.9 = (f32[128,128]{1,0:T(8,128)S(1)}, f32[128,128]{1,0:T(8,128)S(1)}, u32[]{:S(2)}, u32[]{:S(2)}) collective-permute-start(f32[128,128]{1,0:T(8,128)S(1)} %slice_bitcast_fusion.16), channel_id=1, source_target_pairs={{0,32},{32,64},{64,96},{96,128},{128,160},{160,192},{192,224},{1,3... | collective-permute-start | bytes 196616 | tf_op jit(solution)/shard_map/while/body/eval_jaxpr/ppermute | solution.py:29
  250.0 9.1 collective-permute-start.17
  338.9 32.0 %collective-permute-start.9 = (f32[128,128]{1,0:T(8,128)S(1)}, f32[128,128]{1,0:T(8,128)S(1)}, u32[]{:S(2)}, u32[]{:S(2)}) collective-permute-start(f32[128,128]{1,0:T(8,128)S(1)} %slice_bitcast_fusion.16), channel_id=1, source_target_pairs={{0,32},{32,64},{64,96},{96,128},{128,160},{160,192},{192,224},{1,3... | collective-permute-start | bytes 196616 | tf_op jit(solution)/shard_map/while/body/eval_jaxpr/ppermute | solution.py:29
  401.4 9.1 collective-permute-start.17
  420.4 9.1 collective-permute-start.21
  445.4 9.1 collective-permute-start.13
  464.6 9.1 collective-permute-start.17
  493.3 25.8 %collective-permute-start.9 = (f32[128,128]{1,0:T(8,128)S(1)}, f32[128,128]{1,0:T(8,128)S(1)}, u32[]{:S(2)}, u32[]{:S(2)}) collective-permute-start(f32[128,128]{1,0:T(8,128)S(1)} %slice_bitcast_fusion.16), channel_id=1, source_target_pairs={{0,32},{32,64},{64,96},{96,128},{128,160},{160,192},{192,224},{1,3... | collective-permute-start | bytes 196616 | tf_op jit(solution)/shard_map/while/body/eval_jaxpr/ppermute | solution.py:29
  529.1 9.1 collective-permute-start.13
  548.0 9.1 collective-permute-start.17
  591.9 9.1 collective-permute-start.13
  610.9 9.1 collective-permute-start.17
  629.9 9.1 collective-permute-start.21
  639.5 28.4 %collective-permute-start = (f32[128,128]{1,0:T(8,128)S(1)}, f32[128,128]{1,0:T(8,128)S(1)}, u32[]{:S(2)}, u32[]{:S(2)}) collective-permute-start(f32[128,128]{1,0:T(8,128)S(1)} %slice_bitcast_fusion.13), channel_id=1, source_target_pairs={{32,0},{64,32},{96,64},{128,96},{160,128},{192,160},{224,192},{33,... | collective-permute-start | bytes 196616 | tf_op jit(solution)/shard_map/while/body/eval_jaxpr/ppermute | solution.py:29
  677.8 9.1 collective-permute-start.4
  697.0 9.1 collective-permute-start.8
  725.4 9.1 collective-permute-start.4
  744.3 9.1 collective-permute-start.8
  754.0 25.8 %collective-permute-start = (f32[128,128]{1,0:T(8,128)S(1)}, f32[128,128]{1,0:T(8,128)S(1)}, u32[]{:S(2)}, u32[]{:S(2)}) collective-permute-start(f32[128,128]{1,0:T(8,128)S(1)} %slice_bitcast_fusion.13), channel_id=1, source_target_pairs={{32,0},{64,32},{96,64},{128,96},{160,128},{192,160},{224,192},{33,... | collective-permute-start | bytes 196616 | tf_op jit(solution)/shard_map/while/body/eval_jaxpr/ppermute | solution.py:29
  789.8 9.1 collective-permute-start.4
  808.7 9.1 collective-permute-start.8
  836.7 9.1 collective-permute-start.4
  855.7 9.1 collective-permute-start.8
  865.4 28.5 %collective-permute-start = (f32[128,128]{1,0:T(8,128)S(1)}, f32[128,128]{1,0:T(8,128)S(1)}, u32[]{:S(2)}, u32[]{:S(2)}) collective-permute-start(f32[128,128]{1,0:T(8,128)S(1)} %slice_bitcast_fusion.13), channel_id=1, source_target_pairs={{32,0},{64,32},{96,64},{128,96},{160,128},{192,160},{224,192},{33,... | collective-permute-start | bytes 196616 | tf_op jit(solution)/shard_map/while/body/eval_jaxpr/ppermute | solution.py:29
  980.3 25.4 %collective-permute-start = (f32[128,128]{1,0:T(8,128)S(1)}, f32[128,128]{1,0:T(8,128)S(1)}, u32[]{:S(2)}, u32[]{:S(2)}) collective-permute-start(f32[128,128]{1,0:T(8,128)S(1)} %slice_bitcast_fusion.13), channel_id=1, source_target_pairs={{32,0},{64,32},{96,64},{128,96},{160,128},{192,160},{224,192},{33,... | collective-permute-start | bytes 196616 | tf_op jit(solution)/shard_map/while/body/eval_jaxpr/ppermute | solution.py:29
  1015.6 9.1 collective-permute-start.4
  1034.5 9.1 collective-permute-start.8
  1044.3 231.2 %collective-permute-start = (f32[128,128]{1,0:T(8,128)S(1)}, f32[128,128]{1,0:T(8,128)S(1)}, u32[]{:S(2)}, u32[]{:S(2)}) collective-permute-start(f32[128,128]{1,0:T(8,128)S(1)} %slice_bitcast_fusion.13), channel_id=1, source_target_pairs={{32,0},{64,32},{96,64},{128,96},{160,128},{192,160},{224,192},{33,... | collective-permute-start | bytes 196616 | tf_op jit(solution)/shard_map/while/body/eval_jaxpr/ppermute | solution.py:29
  1322.2 9.1 collective-permute-start.8
  (149 other events, 887.8 us)
where the time goes:
time: 1350 us
  waiting for transfers between devices  699 us (52%)
  starting transfers between devices  559 us (41%)
  matrix products  61.5 us (5%)
  other arithmetic  14.5 us (1%)
    ppermute x17, waiting for transfers between devices, passed_along(): lax.ppermute(value, axis, [(source, source + steps) for source in range(f...  364 us
    ppermute x82, waiting for transfers between devices, extended_2(): lax.ppermute(tail, axis, [(i, (i + 1) % count) for i in range(ends)])  316 us
    ppermute x82, starting transfers between devices, extended_2(): lax.ppermute(tail, axis, [(i, (i + 1) % count) for i in range(ends)])  246 us
    ppermute x82, starting transfers between devices, extended_2(): lax.ppermute(head, axis, [((i + 1) % count, i) for i in range(ends)])  202 us
    ppermute x17, starting transfers between devices, passed_along(): lax.ppermute(value, axis, [(source, source + steps) for source in range(f...  111 us
    dot_general x4, matrix products, relax_plane(): jnp.einsum('xij,xj->xi', inverse_rows, residual, precision=exact_mode)  61.5 us
  transfers between devices with their start and end apart: 181, of which 140 were waited for; matrix products, arithmetic and copies ran while one was open for 0% of the time, Pallas kernels for 0%

commit v1 on v0

v1 whole, which is shorter than its diff:
```python
import functools

import jax
import jax.numpy as jnp
from jax import lax
from jax.experimental import pallas as pl
from jax.experimental.pallas import tpu as pltpu
from jax.sharding import PartitionSpec as P

MESH = pl.DeviceIdType.MESH
F32 = jnp.float32
OWN = 16
HALO = 8
SPAN = 32
STEPS = 4
NZ = 16
SHIFTS = range(-3, 4)


def roll(value, shift, axis=1):
    size = value.shape[axis]
    shift = shift % size
    return value if shift == 0 else pltpu.roll(value, shift, axis)


def kernel(
    n, gx, gy, depth,
    v_in, s_in, b_in, out,
    v_rows, s_rows, b_rows, blocks, old, src, fresh, halo, base,
    e_tmp, e_send, e_recv, t_send, t_recv, e_old, coef, given, rows2, imp, resp, out_rows,
    field_send, field_recv, b_recv, b_send, e_ssem, e_rsem, t_ssem, t_rsem, u_ssem, u_rsem, o_ssem, o_rsem,
):
    g, a, q = lax.axis_index("gz"), lax.axis_index("gx"), lax.axis_index("gy")
    par = lax.rem(a, 2)
    local = OWN * n

    def flip(p):
        return p + par * (n - 1 - 2 * p)

    p = flip(g)
    a_left, a_right = lax.rem(a + gx - 1, gx), lax.rem(a + 1, gx)
    step_up = 1 - 2 * par
    first, last = p == 0, p == n - 1
    left = (jnp.where(first, g, g - step_up), jnp.where(first, a_left, a))
    right = (jnp.where(last, g, g + step_up), jnp.where(last, a_right, a))
    places = (left, (g, a), right)

    def remote(source, target, send, recv, device):
        return pltpu.make_async_remote_copy(
            src_ref=source, dst_ref=target, send_sem=send, recv_sem=recv, device_id=device, device_id_type=MESH
        )

    def b_local(source_line, row, count, sem):
        return pltpu.make_async_copy(
            b_in.at[pl.ds(pl.multiple_of(source_line * 128, 128), count * 128)],
            b_rows.at[pl.ds(row * 128, count * 128)], sem,
        )

    b_local(OWN * p, HALO, OWN, b_recv.at[0]).start()

    @pl.when(p > 0)
    def _():
        b_local(OWN * p - HALO, 0, HALO, b_recv.at[1]).start()

    @pl.when(p < n - 1)
    def _():
        b_local(OWN * p + OWN, HALO + OWN, HALO, b_recv.at[2]).start()

    barrier = pltpu.get_barrier_semaphore()

    def greet(i, carry):
        g2, a2 = lax.rem(i, n), lax.rem(a + gx - 1 + i // n, gx)

        @pl.when(jnp.logical_or(g2 != g, a2 != a))
        def _():
            pl.semaphore_signal(barrier, inc=1, device_id=(g2, a2, q), device_id_type=MESH)

        return carry

    lax.fori_loop(0, 3 * n, greet, 0)
    for place in places:
        for k in range(1, gy):
            pl.semaphore_signal(
                barrier, inc=1, device_id=(place[0], place[1], lax.rem(q + k, gy)), device_id_type=MESH
            )
    pl.semaphore_wait(barrier, 3 * n - 1 + 3 * (gy - 1))

    fields = ((v_in, v_rows), (s_in, s_rows))
    planes = pl.ds(depth * g, depth)

    def field_copies(start):
        for other in range(n):
            lo, hi = max(0, OWN * other - HALO), min(local, OWN * other + OWN + HALO)
            row = lo - (OWN * other - HALO)
            target = flip(other)
            for f, (source, place) in enumerate(fields):
                args = (source.at[:, pl.ds(lo, hi - lo), :], place.at[planes, pl.ds(row, hi - lo), :])

                @pl.when(target != g)
                def _():
                    copy = remote(*args, field_send.at[f, other], field_recv.at[f], (target, a, q))
                    if start:
                        copy.start()
                    else:
                        copy.wait_send()

                if start:
                    @pl.when(target == g)
                    def _():
                        pltpu.make_async_copy(*args, field_recv.at[f]).start()

        for f, (source, place) in enumerate(fields):
            ends = (
                (local - HALO, 0, (flip(n - 1), a_right, q), n),
                (0, HALO + OWN, (flip(0), a_left, q), n + 1),
            )
            for line, row, device, sem in ends:
                copy = remote(
                    source.at[:, pl.ds(line, HALO), :], place.at[planes, pl.ds(row, HALO), :],
                    field_send.at[f, sem], field_recv.at[f], device,
                )
                if start:
                    copy.start()
                else:
                    copy.wait_send()

    field_copies(True)

    def b_remote(start):
        for cond, line, row, device, recv, send in (
            (last, local - HALO, 0, right, 1, 0), (first, 0, HALO + OWN, left, 2, 1),
        ):
            @pl.when(cond)
            def _():
                copy = remote(
                    b_in.at[pl.ds(line * 128, HALO * 128)], b_rows.at[pl.ds(row * 128, HALO * 128)],
                    b_send.at[send], b_recv.at[recv], (device[0], device[1], q),
                )
                if start:
                    copy.start()
                else:
                    copy.wait_send()

    b_remote(True)

    lane = lax.broadcasted_iota(jnp.int32, (SPAN, 128), 1)
    row = lax.broadcasted_iota(jnp.int32, (SPAN, 128), 0)
    group, xlane = lane // SPAN, lane % SPAN
    line = local * a + OWN * p - HALO + xlane
    inside = jnp.logical_and(line >= 0, line < local * gx)
    low_half, even = group < 2, group % 2 == 0
    top_cell, bottom_cell = jnp.logical_and(row == 0, group == 0), jnp.logical_and(row == SPAN - 1, group == 3)
    inside1, group1, xlane1 = inside[:1], group[:1], xlane[:1]
    group8, xlane8 = group[:8], xlane[:8]
    mine8 = jnp.logical_and(group8 == q, jnp.logical_and(xlane8 >= HALO, xlane8 < HALO + OWN))
    mine1 = mine8[:1]

    def y_sum(cells):
        up = jnp.where(group1 == 0, 0.0, roll(cells[SPAN - 1 :], SPAN))
        down = jnp.where(group1 == 3, 0.0, roll(cells[:1], -SPAN))
        return cells + jnp.where(row == 0, up, roll(cells, 1, 0)) + jnp.where(row == SPAN - 1, down, roll(cells, -1, 0))

    def box(cells):
        return y_sum(cells + roll(cells, 1) + roll(cells, -1))

    def apply(residual):
        acc = blocks[0] * residual[:1]
        for j in range(1, SPAN):
            acc = acc + blocks[j] * residual[j : j + 1]
        a0, a1, a2, a3 = (acc[SPAN * i : SPAN * (i + 1)] for i in range(4))
        b0 = jnp.where(low_half, a0, a2) + roll(jnp.where(low_half, a2, a0), 64)
        b1 = jnp.where(low_half, a1, a3) + roll(jnp.where(low_half, a3, a1), 64)
        other = jnp.where(even, b1, b0)
        return jnp.where(even, b0 + roll(other, -SPAN), b1 + roll(other, SPAN))

    b_local(0, HALO, OWN, b_recv.at[0]).wait()
    b_local(0, 0, HALO, b_recv.at[1]).wait()
    b_local(0, HALO + OWN, HALO, b_recv.at[2]).wait()

    def turn(x, carry):
        rows = pl.ds(pl.multiple_of(x * 128, 128), 128)
        b_rows[rows, :] = b_rows[rows, :].T
        return carry

    lax.fori_loop(0, SPAN, turn, 0)

    def gather(j, carry):
        parts = [b_rows[pl.ds(SPAN * jg + j, SPAN, stride=128), :] for jg in range(4)]
        blocks[j] = jnp.concatenate(parts, axis=0).T
        return carry

    lax.fori_loop(0, SPAN, gather, 0)

    cells = []
    for slot, at in ((0, 0), (SPAN - 1, 3)):
        column = jnp.zeros((SPAN, 128), F32)
        for i in range(4):
            column = jnp.where(group == i, roll(blocks[slot, SPAN * i : SPAN * (i + 1), :], SPAN * (i - at)), column)
        cells.append(y_sum(jnp.where(inside, column, 0.0)))
    for j in range(SPAN):
        rows2[0, j : j + 1, :] = blocks[j, :1, :]
        rows2[1, j : j + 1, :] = blocks[j, 127:, :]
    for e in range(2):
        for d in range(3):
            imp[3 * e + d] = roll(cells[e], -(d - 1))

    def respond(i, carry):
        resp[i] = y_sum(jnp.where(inside, apply(imp[i]), 0.0))
        return carry

    lax.fori_loop(0, 6, respond, 0)

    def keep(index, value):
        total = value + roll(value, 32)
        total = total + roll(total, 64)
        t_send[index : index + 1, :] = jnp.where(mine1, total, 0.0)

    def dot(e, value):
        return jnp.sum(rows2[e] * value, axis=0, keepdims=True)

    t_send[32:40, :] = jnp.zeros((8, 128), F32)
    for e in range(2):
        keep(2 * e, jnp.where(group1 == 0, rows2[e, :1, :], 0.0))
        keep(2 * e + 1, jnp.where(group1 == 3, rows2[e, SPAN - 1 :, :], 0.0))
        for f in range(2):
            for d in range(-1, 2):
                keep(4 + (2 * e + f) * 3 + d + 1, dot(e, roll(cells[f], -d)))
            for d in range(-2, 3):
                total = None
                for near in range(-1, 2):
                    far = d - near
                    if abs(far) <= 1:
                        term = roll(resp[3 * f + far + 1], -near)
                        total = term if total is None else total + term
                keep(16 + (2 * e + f) * 5 + d + 2, dot(e, total))

    whole = v_rows
    for f, (place, rows_ref) in enumerate(((old, v_rows), (src, s_rows))):
        pltpu.make_async_copy(rows_ref, rows_ref, field_recv.at[f]).wait()
        for w in range(NZ // 4):
            turned = rows_ref[4 * w : 4 * w + 4].reshape(128, 128).T
            for k in range(4):
                tile = jnp.zeros((SPAN, 128), F32)
                for i in range(4):
                    tile = jnp.where(group == i, roll(turned[SPAN * i : SPAN * (i + 1)], SPAN * (i - k)), tile)
                place[4 * w + k] = jnp.where(inside, tile, 0.0)
    zero_tile = jnp.zeros((SPAN, 128), F32)
    old[NZ] = zero_tile
    old[2 * NZ + 1] = zero_tile
    e_old[NZ] = jnp.zeros((8, 128), F32)
    e_old[2 * NZ + 1] = jnp.zeros((8, 128), F32)

    def own_edges(value, e):
        shift = SPAN * q if e == 0 else SPAN * (q + 1)
        return jnp.where(mine8, pltpu.roll(value, lax.rem(shift, 128), 1), 0.0)

    for z in range(NZ):
        e_tmp[z : z + 1, :] = old[z, :1, :]
        e_tmp[NZ + z : NZ + z + 1, :] = old[z, SPAN - 1 :, :]
    for k in range(4):
        t_send[40 + 8 * k : 48 + 8 * k, :] = own_edges(e_tmp[8 * k : 8 * k + 8, :], k // 2)

    def edge_copies(source, target, send, recv, start):
        for x, place in enumerate(places):
            for k in range(gy):
                if x == 1 and k == 0:
                    if start:
                        pltpu.make_async_copy(source, target.at[1, q], recv).start()
                    continue
                copy = remote(
                    source, target.at[2 - x, q], send.at[3 * k + x], recv, (place[0], place[1], lax.rem(q + k, gy))
                )
                if start:
                    copy.start()
                else:
                    copy.wait_send()

    edge_copies(t_send, t_recv, t_ssem, t_rsem, True)

    def gathered(ref, rows):
        sides = []
        for x in range(3):
            total = ref[x, 0, rows, :]
            for k in range(1, gy):
                total = total + ref[x, k, rows, :]
            sides.append(total)
        return jnp.where(
            xlane8 < HALO, roll(sides[0], -OWN), jnp.where(xlane8 >= HALO + OWN, roll(sides[2], OWN), sides[1])
        )

    def halo_copy(window, side, start):
        device = places[2 * side]
        device = (device[0], device[1], q)
        at = STEPS * window

        @pl.when(window < 4)
        def _():
            copy = remote(
                fresh.at[pl.ds(at, STEPS)], halo.at[window, 1 - side],
                u_ssem.at[window, side], u_rsem.at[window, 1 - side], device,
            )
            if start:
                copy.start()
            else:
                copy.wait_send()

        @pl.when(window >= 4)
        def _():
            copy = remote(
                fresh.at[at + STEPS - 1], halo.at[window, 1 - side, STEPS - 1],
                u_ssem.at[window, side], u_rsem.at[window, 1 - side], device,
            )
            if start:
                copy.start()
            else:
                copy.wait_send()

    def halo_wait(window):
        @pl.when(window < 4)
        def _():
            for side in range(2):
                ref = halo.at[window, side]
                pltpu.make_async_copy(ref, ref, u_rsem.at[window, side]).wait()

        @pl.when(window >= 4)
        def _():
            for side in range(2):
                ref = halo.at[window, side, STEPS - 1]
                pltpu.make_async_copy(ref, ref, u_rsem.at[window, side]).wait()

    def out_copy(z, start):
        owner = z // depth
        source = out_rows.at[z]
        target = out.at[lax.rem(z, depth), pl.ds(pl.multiple_of(OWN * p, OWN), OWN), :]

        @pl.when(owner != g)
        def _():
            copy = remote(source, target, o_ssem.at[z], o_rsem, (owner, a, q))
            if start:
                copy.start()
            else:
                copy.wait_send()

        if start:
            @pl.when(owner == g)
            def _():
                pltpu.make_async_copy(source, target, o_rsem).start()

    def window_step(window, carry):
        backward = window // 4
        m0 = STEPS * (window - 4 * backward)
        at = (NZ + 1) * backward + m0
        t0 = STEPS * window
        opening = m0 == 0

        def source_plane(m):
            return src[m + backward * (NZ - 1 - 2 * m)]

        @pl.when(opening)
        def _():
            base[0] = zero_tile

        @pl.when(jnp.logical_not(opening))
        def _():
            base[0] = fresh[jnp.maximum(t0 - 1, 0)]

        def base_step(t, before):
            cell = old[at + t]
            residual = source_plane(m0 + t) - 27.0 * cell + box(cell + old[at + t + 1] + before)
            now = jnp.where(inside, cell + apply(residual), 0.0)
            base[t + 1] = now
            return now

        lax.fori_loop(0, STEPS - 1, base_step, base[0])

        @pl.when(window == 0)
        def _():
            e_tmp[...] = jnp.zeros(e_tmp.shape, F32)

        @pl.when(window > 0)
        def _():
            for t in range(STEPS):
                tile = fresh.at[jnp.maximum(t0 - STEPS + t, 0)]
                e_tmp[t : t + 1, :] = tile[:1, :]
                e_tmp[8 + t : 9 + t, :] = tile[SPAN - 1 :, :]

        for t in range(1, STEPS):
            e_tmp[3 + t : 4 + t, :] = base[t, :1, :]
            e_tmp[11 + t : 12 + t, :] = base[t, SPAN - 1 :, :]
        for e in range(2):
            e_send[window, 8 * e : 8 * e + 8, :] = own_edges(e_tmp[8 * e : 8 * e + 8, :], e)
        edge_copies(e_send.at[window], e_recv.at[window], e_ssem.at[window], e_rsem.at[window], True)

        @pl.when(window == 0)
        def _():
            pltpu.make_async_copy(t_recv, t_recv, t_rsem).wait()
            for k in range(9):
                part = jnp.where(inside[:8], gathered(t_recv, slice(8 * k, 8 * k + 8)), 0.0)
                if k < 5:
                    coef[8 * k : 8 * k + 8, :] = part
                else:
                    e = (k - 5) // 2
                    for r in range(8):
                        e_old[8 * ((k - 5) % 2) + r, e : e + 1, :] = part[r : r + 1]

        arrived = e_recv.at[window]
        pltpu.make_async_copy(arrived, arrived, e_rsem.at[window]).wait()
        edges = [jnp.where(inside[:8], gathered(arrived, slice(8 * e, 8 * e + 8)), 0.0) for e in range(2)]

        @pl.when(jnp.logical_and(window > 0, window <= 4))
        def _():
            for t in range(STEPS):
                for e in range(2):
                    e_old[2 * NZ - jnp.maximum(t0 - STEPS + t, 0), e : e + 1, :] = edges[e][t : t + 1]

        before = [jnp.where(opening, 0.0, edges[e][STEPS - 1 : STEPS]) for e in range(2)]
        gives = []
        for t in range(STEPS):
            total = [
                before[e] + (e_old[at + t, e : e + 1, :] + e_old[at + t + 1, e : e + 1, :]) for e in range(2)
            ]
            from_low = [roll(total[1], SPAN - c) for c in SHIFTS]
            from_high = [roll(total[0], -SPAN - c) for c in SHIFTS]
            give = {}
            for d in range(-2, 3):
                k = d + 3
                give[0, d] = jnp.where(group1 > 0, from_low[k - 1] + from_low[k] + from_low[k + 1], 0.0)
                give[1, d] = jnp.where(group1 < gy - 1, from_high[k - 1] + from_high[k] + from_high[k + 1], 0.0)
            gives.append(give)
            given[t, 0:1, :] = pltpu.roll(give[0, 0], lax.rem(128 - SPAN * q, 128), 1)
            given[t, 1:2, :] = pltpu.roll(give[1, 0], SPAN * (3 - q), 1)
            if t == STEPS - 1:
                break
            before = []
            for e in range(2):
                value = edges[e][STEPS + t : STEPS + t + 1]
                for s in range(t + 1):
                    lag = t - s
                    first_row = (0, 4, 16)[lag]
                    for f in range(2):
                        for d in range(-lag, lag + 1):
                            r = first_row + (2 * e + f) * (2 * lag + 1) + d + lag
                            value = value + coef[r : r + 1, :] * gives[s][f, d]
                before.append(jnp.where(inside1, value, 0.0))

        @pl.when(window > 0)
        def _():
            halo_wait(window - 1)

        def merged(t):
            mid = fresh[jnp.maximum(t0 - STEPS + t, 0)]
            w = jnp.maximum(window - 1, 0)
            tile = jnp.where(
                xlane < HALO, roll(halo[w, 0, t], -OWN),
                jnp.where(xlane >= HALO + OWN, roll(halo[w, 1, t], OWN), mid),
            )
            return jnp.where(inside, tile, 0.0)

        @pl.when(jnp.logical_and(window > 0, window <= 4))
        def _():
            for t in range(STEPS):
                old[2 * NZ - jnp.maximum(t0 - STEPS + t, 0)] = merged(t)

        @pl.when(jnp.logical_not(opening))
        def _():
            base[0] = merged(STEPS - 1)

        def true_step(t, before):
            cell = old[at + t]
            residual = source_plane(m0 + t) - 27.0 * cell + box(cell + old[at + t + 1] + before)
            residual = residual + jnp.where(top_cell, given[t, 0:1, :], 0.0)
            residual = residual + jnp.where(bottom_cell, given[t, 1:2, :], 0.0)
            now = jnp.where(inside, cell + apply(residual), 0.0)
            fresh[t0 + t] = now

            @pl.when(backward == 0)
            def _():
                old[2 * NZ - jnp.minimum(t0 + t, NZ - 1)] = now

            return now

        lax.fori_loop(0, STEPS, true_step, base[0])

        @pl.when(window < 7)
        def _():
            halo_copy(window, 0, True)
            halo_copy(window, 1, True)

        @pl.when(backward == 1)
        def _():
            tiles = [fresh[t0 + k] for k in range(4)]
            parts = []
            for i in range(4):
                part = tiles[0] if i == 0 else roll(tiles[0], -SPAN * i)
                for k in range(1, 4):
                    part = jnp.where(group == k, roll(tiles[k], SPAN * (k - i)), part)
                parts.append(part)
            lines = jnp.concatenate(parts, axis=0).T
            for k in range(4):
                z = jnp.maximum(2 * NZ - 1 - t0 - k, 0)
                out_rows[z] = lines[SPAN * k + HALO : SPAN * k + HALO + OWN]
                out_copy(z, True)

        return carry

    lax.fori_loop(0, 8, window_step, 0)

    field_copies(False)
    b_remote(False)
    edge_copies(t_send, t_recv, t_ssem, t_rsem, False)

    def drain(window, carry):
        edge_copies(e_send.at[window], e_recv.at[window], e_ssem.at[window], e_rsem.at[window], False)

        @pl.when(window < 7)
        def _():
            halo_copy(window, 0, False)
            halo_copy(window, 1, False)

        return carry

    lax.fori_loop(0, 8, drain, 0)

    def drain_out(z, carry):
        out_copy(z, False)
        return carry

    lax.fori_loop(0, NZ, drain_out, 0)
    pltpu.make_async_copy(out, out, o_rsem).wait()


def solution(mesh):
    n, gx, gy = mesh.shape["gz"], mesh.shape["gx"], mesh.shape["gy"]

    def body(initial_field, source_term, block_inverse):
        depth, local, width = initial_field.shape
        vmem = lambda *shape: pltpu.VMEM(shape, F32)
        dma = pltpu.SemaphoreType.DMA
        return pl.pallas_call(
            functools.partial(kernel, n, gx, gy, depth),
            out_shape=jax.ShapeDtypeStruct(initial_field.shape, F32),
            in_specs=[pl.BlockSpec(memory_space=pl.ANY)] * 3,
            out_specs=pl.BlockSpec(memory_space=pltpu.VMEM),
            scratch_shapes=[
                vmem(NZ, SPAN, 128), vmem(NZ, SPAN, 128), vmem(SPAN * 128, 128), vmem(SPAN, 128, 128),
                vmem(2 * NZ + 2, SPAN, 128), vmem(NZ, SPAN, 128), vmem(2 * NZ, SPAN, 128),
                vmem(8, 2, STEPS, SPAN, 128), vmem(STEPS, SPAN, 128),
                vmem(2 * NZ, 128), vmem(8, 16, 128), vmem(8, 3, gy, 16, 128), vmem(72, 128), vmem(3, gy, 72, 128),
                vmem(2 * NZ + 2, 8, 128), vmem(40, 128), vmem(STEPS, 8, 128), vmem(2, SPAN, 128),
                vmem(6, SPAN, 128), vmem(6, SPAN, 128), vmem(NZ, OWN, 128),
                dma((2, n + 2)), dma((2,)), dma((3,)), dma((2,)),
                dma((8, 3 * gy)), dma((8,)), dma((3 * gy,)), dma,
                dma((8, 2)), dma((8, 2)), dma((NZ,)), dma,
            ],
            compiler_params=pltpu.CompilerParams(
                collective_id=0, has_side_effects=True, vmem_limit_bytes=40 * 1024 * 1024
            ),
        )(initial_field, source_term, block_inverse.reshape(local * width, width))

    return jax.shard_map(
        body, mesh=mesh,
        in_specs=(P("gz", "gx", "gy"), P("gz", "gx", "gy"), P("gx", "gy", None)),
        out_specs=P("gz", "gx", "gy"), check_vma=False,
    )
```

time: 1350 us -> 121 us (0.09)
  the two profiles are of different devices: /device:TPU:166 before, /device:TPU:1 now
where the time goes in v1:
time: 121 us
  Pallas kernels  115 us (95%)
  local copies, waits for them, and re-layouts  5.85 us (5%)
    pallas_call x1, Pallas kernels, body(): pl.pallas_call(functools.partial(kernel, n, gx, gy, depth), out_shape=jax...  115 us
    unnamed x7, local copies, waits for them, and re-layouts  5.85 us

profile of v1, /device:TPU:1, one launch (start us, length us, event | category | flops | bytes accessed | tf_op | source)
XLA Modules:
  0.0 120.5 jit_solution(16712900169061913788)
XLA Ops:
  0.0 0.0 copy-start
  0.0 3.4 %copy-done = f32[128,128,128]{2,1,0:T(8,128)S(1)} copy-done((f32[128,128,128]{2,1,0:T(8,128)S(1)}, f32[128,128,128]{2,1,0:T(8,128)}, u32[]{:S(2)}) %copy-start) | copy-done | bytes 8388632
  3.4 0.0 copy-start.1
  3.4 0.9 copy-done.1
  4.3 0.0 copy-start.2
  4.3 0.9 copy-done.2
  5.2 114.7 %shard_map.37 = f32[2,128,128]{2,1,0:T(8,128)S(1)} custom-call(f32[2,128,128]{2,1,0:T(8,128)S(1)} %copy-done.1, f32[2,128,128]{2,1,0:T(8,128)S(1)} %copy-done.2, f32[16384,128]{1,0:T(8,128)S(1)} %bitcast.1), custom_call_target="tpu_custom_call" | custom-call | tf_op jit(solution)/shard_map/pallas_call | solution.py:539
  119.9 0.7 copy.5
Async XLA Ops:
  0.0 3.4 %copy-start = (f32[128,128,128]{2,1,0:T(8,128)S(1)}, f32[128,128,128]{2,1,0:T(8,128)}, u32[]{:S(2)}) copy-start(f32[128,128,128]{2,1,0:T(8,128)} %param.5) | copy-start | bytes 25165828
  3.4 0.9 copy-start.1
  4.3 0.9 copy-start.2

commit v2 on v1

--- a/solution.py
+++ b/solution.py
@@ -14,7 +14,6 @@
 SPAN = 32
 STEPS = 4
 NZ = 16
-SHIFTS = range(-3, 4)
 
 
 def roll(value, shift, axis=1):
@@ -27,7 +26,7 @@
     n, gx, gy, depth,
     v_in, s_in, b_in, out,
     v_rows, s_rows, b_rows, blocks, old, src, fresh, halo, base,
-    e_tmp, e_send, e_recv, t_send, t_recv, e_old, coef, given, rows2, imp, resp, out_rows,
+    free, e_send, e_recv, t_send, t_recv, e_old, coef, rows2, imp, resp, out_rows,
     field_send, field_recv, b_recv, b_send, e_ssem, e_rsem, t_ssem, t_rsem, u_ssem, u_rsem, o_ssem, o_rsem,
 ):
     g, a, q = lax.axis_index("gz"), lax.axis_index("gx"), lax.axis_index("gy")
@@ -124,24 +123,21 @@
                 else:
                     copy.wait_send()
 
+    share = HALO // n
+
+    def b_remote(start):
+        for side, line, row, device in (
+            (0, local - HALO, 0, (flip(n - 1), a_right, q)), (1, 0, HALO + OWN, (flip(0), a_left, q)),
+        ):
+            rows = lambda at: pl.ds(pl.multiple_of((at + share * g) * 128, 128), share * 128)
+            copy = remote(b_in.at[rows(line)], b_rows.at[rows(row)], b_send.at[side], b_recv.at[1 + side], device)
+            if start:
+                copy.start()
+            else:
+                copy.wait_send()
+
+    b_remote(True)
     field_copies(True)
-
-    def b_remote(start):
-        for cond, line, row, device, recv, send in (
-            (last, local - HALO, 0, right, 1, 0), (first, 0, HALO + OWN, left, 2, 1),
-        ):
-            @pl.when(cond)
-            def _():
-                copy = remote(
-                    b_in.at[pl.ds(line * 128, HALO * 128)], b_rows.at[pl.ds(row * 128, HALO * 128)],
-                    b_send.at[send], b_recv.at[recv], (device[0], device[1], q),
-                )
-                if start:
-                    copy.start()
-                else:
-                    copy.wait_send()
-
-    b_remote(True)
 
     lane = lax.broadcasted_iota(jnp.int32, (SPAN, 128), 1)
     row = lax.broadcasted_iota(jnp.int32, (SPAN, 128), 0)
@@ -149,11 +145,10 @@
     line = local * a + OWN * p - HALO + xlane
     inside = jnp.logical_and(line >= 0, line < local * gx)
     low_half, even = group < 2, group % 2 == 0
-    top_cell, bottom_cell = jnp.logical_and(row == 0, group == 0), jnp.logical_and(row == SPAN - 1, group == 3)
-    inside1, group1, xlane1 = inside[:1], group[:1], xlane[:1]
-    group8, xlane8 = group[:8], xlane[:8]
-    mine8 = jnp.logical_and(group8 == q, jnp.logical_and(xlane8 >= HALO, xlane8 < HALO + OWN))
-    mine1 = mine8[:1]
+    group1 = group[:1]
+    group8, xlane8, inside8, sub8 = group[:8], xlane[:8], inside[:8], row[:8]
+    ends8 = jnp.logical_and(jnp.logical_or(sub8 == 0, sub8 == 7), jnp.logical_and(xlane8 >= HALO, xlane8 < HALO + OWN))
+    top8, bottom8 = jnp.logical_and(sub8 == 0, group8 == 0), jnp.logical_and(sub8 == 7, group8 == 3)
 
     def y_sum(cells):
         up = jnp.where(group1 == 0, 0.0, roll(cells[SPAN - 1 :], SPAN))
@@ -173,30 +168,33 @@
         other = jnp.where(even, b1, b0)
         return jnp.where(even, b0 + roll(other, -SPAN), b1 + roll(other, SPAN))
 
-    b_local(0, HALO, OWN, b_recv.at[0]).wait()
-    b_local(0, 0, HALO, b_recv.at[1]).wait()
-    b_local(0, HALO + OWN, HALO, b_recv.at[2]).wait()
-
     def turn(x, carry):
         rows = pl.ds(pl.multiple_of(x * 128, 128), 128)
         b_rows[rows, :] = b_rows[rows, :].T
         return carry
 
-    lax.fori_loop(0, SPAN, turn, 0)
+    b_local(0, HALO, OWN, b_recv.at[0]).wait()
+    lax.fori_loop(HALO, HALO + OWN, turn, 0, unroll=4)
+    b_local(0, 0, HALO, b_recv.at[1]).wait()
+    lax.fori_loop(0, HALO, turn, 0, unroll=4)
+    b_local(0, HALO + OWN, HALO, b_recv.at[2]).wait()
+    lax.fori_loop(HALO + OWN, SPAN, turn, 0, unroll=4)
 
     def gather(j, carry):
         parts = [b_rows[pl.ds(SPAN * jg + j, SPAN, stride=128), :] for jg in range(4)]
         blocks[j] = jnp.concatenate(parts, axis=0).T
         return carry
 
-    lax.fori_loop(0, SPAN, gather, 0)
-
-    cells = []
+    lax.fori_loop(0, SPAN, gather, 0, unroll=4)
+
+    columns, cells = [], []
     for slot, at in ((0, 0), (SPAN - 1, 3)):
         column = jnp.zeros((SPAN, 128), F32)
         for i in range(4):
             column = jnp.where(group == i, roll(blocks[slot, SPAN * i : SPAN * (i + 1), :], SPAN * (i - at)), column)
-        cells.append(y_sum(jnp.where(inside, column, 0.0)))
+        columns.append(jnp.where(inside, column, 0.0))
+        cells.append(y_sum(columns[-1]))
+    resp[6], resp[7] = columns
     for j in range(SPAN):
         rows2[0, j : j + 1, :] = blocks[j, :1, :]
         rows2[1, j : j + 1, :] = blocks[j, 127:, :]
@@ -210,31 +208,46 @@
 
     lax.fori_loop(0, 6, respond, 0)
 
-    def keep(index, value):
+    def spread(value):
         total = value + roll(value, 32)
-        total = total + roll(total, 64)
-        t_send[index : index + 1, :] = jnp.where(mine1, total, 0.0)
-
-    def dot(e, value):
-        return jnp.sum(rows2[e] * value, axis=0, keepdims=True)
-
-    t_send[32:40, :] = jnp.zeros((8, 128), F32)
-    for e in range(2):
-        keep(2 * e, jnp.where(group1 == 0, rows2[e, :1, :], 0.0))
-        keep(2 * e + 1, jnp.where(group1 == 3, rows2[e, SPAN - 1 :, :], 0.0))
-        for f in range(2):
-            for d in range(-1, 2):
-                keep(4 + (2 * e + f) * 3 + d + 1, dot(e, roll(cells[f], -d)))
-            for d in range(-2, 3):
-                total = None
-                for near in range(-1, 2):
-                    far = d - near
-                    if abs(far) <= 1:
-                        term = roll(resp[3 * f + far + 1], -near)
-                        total = term if total is None else total + term
-                keep(16 + (2 * e + f) * 5 + d + 2, dot(e, total))
-
-    whole = v_rows
+        return total + roll(total, 64)
+
+    def pair(values):
+        return jnp.where(sub8 == 0, spread(values[0]), spread(values[1]))
+
+    def dots(value):
+        return pair([jnp.sum(rows2[e] * value, axis=0, keepdims=True) for e in range(2)])
+
+    def packed(pairs):
+        tile = None
+        for m in range(0, len(pairs), 4):
+            part = jnp.zeros((8, 128), F32)
+            for k, value in enumerate(pairs[m : m + 4]):
+                part = jnp.where(group8 == k, value, part)
+            part = roll(jnp.where(ends8, part, 0.0), m // 2, 0)
+            tile = part if tile is None else tile + part
+        return tile
+
+    def edge_pair(top, bottom, k):
+        return jnp.where(sub8 == 0, roll(top, SPAN * k), roll(bottom, SPAN * (k - 3)))
+
+    first_pairs = [
+        pair([jnp.where(group1 == 0, rows2[e, :1, :], 0.0) for e in range(2)]),
+        pair([jnp.where(group1 == 3, rows2[e, SPAN - 1 :, :], 0.0) for e in range(2)]),
+    ]
+    coef[0] = packed(first_pairs)
+    later_pairs = [dots(roll(cells[f], -d)) for f in range(2) for d in range(-1, 2)]
+    for f in range(2):
+        for d in range(-2, 3):
+            total = None
+            for near in range(-1, 2):
+                far = d - near
+                if abs(far) <= 1:
+                    term = roll(resp[3 * f + far + 1], -near)
+                    total = term if total is None else total + term
+            later_pairs.append(dots(total))
+    t_send[0] = packed(later_pairs)
+
     for f, (place, rows_ref) in enumerate(((old, v_rows), (src, s_rows))):
         pltpu.make_async_copy(rows_ref, rows_ref, field_recv.at[f]).wait()
         for w in range(NZ // 4):
@@ -244,21 +257,12 @@
                 for i in range(4):
                     tile = jnp.where(group == i, roll(turned[SPAN * i : SPAN * (i + 1)], SPAN * (i - k)), tile)
                 place[4 * w + k] = jnp.where(inside, tile, 0.0)
-    zero_tile = jnp.zeros((SPAN, 128), F32)
+    zero_tile, zero8 = jnp.zeros((SPAN, 128), F32), jnp.zeros((8, 128), F32)
     old[NZ] = zero_tile
     old[2 * NZ + 1] = zero_tile
     e_old[NZ] = jnp.zeros((8, 128), F32)
     e_old[2 * NZ + 1] = jnp.zeros((8, 128), F32)
-
-    def own_edges(value, e):
-        shift = SPAN * q if e == 0 else SPAN * (q + 1)
-        return jnp.where(mine8, pltpu.roll(value, lax.rem(shift, 128), 1), 0.0)
-
-    for z in range(NZ):
-        e_tmp[z : z + 1, :] = old[z, :1, :]
-        e_tmp[NZ + z : NZ + z + 1, :] = old[z, SPAN - 1 :, :]
-    for k in range(4):
-        t_send[40 + 8 * k : 48 + 8 * k, :] = own_edges(e_tmp[8 * k : 8 * k + 8, :], k // 2)
+    t_send[1] = packed([edge_pair(old[z, :8, :], old[z, SPAN - 8 :, :], z % 4) for z in range(NZ)])
 
     def edge_copies(source, target, send, recv, start):
         for x, place in enumerate(places):
@@ -277,16 +281,20 @@
 
     edge_copies(t_send, t_recv, t_ssem, t_rsem, True)
 
-    def gathered(ref, rows):
-        sides = []
-        for x in range(3):
-            total = ref[x, 0, rows, :]
-            for k in range(1, gy):
-                total = total + ref[x, k, rows, :]
-            sides.append(total)
-        return jnp.where(
-            xlane8 < HALO, roll(sides[0], -OWN), jnp.where(xlane8 >= HALO + OWN, roll(sides[2], OWN), sides[1])
-        )
+    def unpacked(ref, at=None):
+        tiles = []
+        for k in range(gy):
+            sides = [ref[x, k] if at is None else ref[x, k, at] for x in range(3)]
+            tiles.append(jnp.where(
+                xlane8 < HALO, roll(sides[0], -OWN), jnp.where(xlane8 >= HALO + OWN, roll(sides[2], OWN), sides[1])
+            ))
+        whole = []
+        for k in range(4):
+            tile = jnp.zeros((8, 128), F32)
+            for b in range(gy):
+                tile = jnp.where(group8 == b, roll(tiles[b], SPAN * (b - k)), tile)
+            whole.append(jnp.where(inside8, tile, 0.0))
+        return lambda i: roll(whole[i % 4], -2 * (i // 4), 0)
 
     def halo_copy(window, side, start):
         device = places[2 * side]
@@ -373,75 +381,13 @@
 
         lax.fori_loop(0, STEPS - 1, base_step, base[0])
 
-        @pl.when(window == 0)
-        def _():
-            e_tmp[...] = jnp.zeros(e_tmp.shape, F32)
-
-        @pl.when(window > 0)
-        def _():
-            for t in range(STEPS):
-                tile = fresh.at[jnp.maximum(t0 - STEPS + t, 0)]
-                e_tmp[t : t + 1, :] = tile[:1, :]
-                e_tmp[8 + t : 9 + t, :] = tile[SPAN - 1 :, :]
-
-        for t in range(1, STEPS):
-            e_tmp[3 + t : 4 + t, :] = base[t, :1, :]
-            e_tmp[11 + t : 12 + t, :] = base[t, SPAN - 1 :, :]
-        for e in range(2):
-            e_send[window, 8 * e : 8 * e + 8, :] = own_edges(e_tmp[8 * e : 8 * e + 8, :], e)
+        guesses = [edge_pair(base[k + 1, :8, :], base[k + 1, SPAN - 8 :, :], k) for k in range(STEPS - 1)]
+        done = []
+        for k in range(STEPS):
+            tile = fresh.at[jnp.maximum(t0 - STEPS + k, 0)]
+            done.append(edge_pair(tile[:8, :], tile[SPAN - 8 :, :], k))
+        e_send[window] = jnp.where(window == 0, coef[0], packed(done)) + packed([zero8] * 4 + guesses)
         edge_copies(e_send.at[window], e_recv.at[window], e_ssem.at[window], e_rsem.at[window], True)
-
-        @pl.when(window == 0)
-        def _():
-            pltpu.make_async_copy(t_recv, t_recv, t_rsem).wait()
-            for k in range(9):
-                part = jnp.where(inside[:8], gathered(t_recv, slice(8 * k, 8 * k + 8)), 0.0)
-                if k < 5:
-                    coef[8 * k : 8 * k + 8, :] = part
-                else:
-                    e = (k - 5) // 2
-                    for r in range(8):
-                        e_old[8 * ((k - 5) % 2) + r, e : e + 1, :] = part[r : r + 1]
-
-        arrived = e_recv.at[window]
-        pltpu.make_async_copy(arrived, arrived, e_rsem.at[window]).wait()
-        edges = [jnp.where(inside[:8], gathered(arrived, slice(8 * e, 8 * e + 8)), 0.0) for e in range(2)]
-
-        @pl.when(jnp.logical_and(window > 0, window <= 4))
-        def _():
-            for t in range(STEPS):
-                for e in range(2):
-                    e_old[2 * NZ - jnp.maximum(t0 - STEPS + t, 0), e : e + 1, :] = edges[e][t : t + 1]
-
-        before = [jnp.where(opening, 0.0, edges[e][STEPS - 1 : STEPS]) for e in range(2)]
-        gives = []
-        for t in range(STEPS):
-            total = [
-                before[e] + (e_old[at + t, e : e + 1, :] + e_old[at + t + 1, e : e + 1, :]) for e in range(2)
-            ]
-            from_low = [roll(total[1], SPAN - c) for c in SHIFTS]
-            from_high = [roll(total[0], -SPAN - c) for c in SHIFTS]
-            give = {}
-            for d in range(-2, 3):
-                k = d + 3
-                give[0, d] = jnp.where(group1 > 0, from_low[k - 1] + from_low[k] + from_low[k + 1], 0.0)
-                give[1, d] = jnp.where(group1 < gy - 1, from_high[k - 1] + from_high[k] + from_high[k + 1], 0.0)
-            gives.append(give)
-            given[t, 0:1, :] = pltpu.roll(give[0, 0], lax.rem(128 - SPAN * q, 128), 1)
-            given[t, 1:2, :] = pltpu.roll(give[1, 0], SPAN * (3 - q), 1)
-            if t == STEPS - 1:
-                break
-            before = []
-            for e in range(2):
-                value = edges[e][STEPS + t : STEPS + t + 1]
-                for s in range(t + 1):
-                    lag = t - s
-                    first_row = (0, 4, 16)[lag]
-                    for f in range(2):
-                        for d in range(-lag, lag + 1):
-                            r = first_row + (2 * e + f) * (2 * lag + 1) + d + lag
-                            value = value + coef[r : r + 1, :] * gives[s][f, d]
-                before.append(jnp.where(inside1, value, 0.0))
 
         @pl.when(window > 0)
         def _():
@@ -465,21 +411,79 @@
         def _():
             base[0] = merged(STEPS - 1)
 
-        def true_step(t, before):
+        for t in range(STEPS):
             cell = old[at + t]
-            residual = source_plane(m0 + t) - 27.0 * cell + box(cell + old[at + t + 1] + before)
-            residual = residual + jnp.where(top_cell, given[t, 0:1, :], 0.0)
-            residual = residual + jnp.where(bottom_cell, given[t, 1:2, :], 0.0)
-            now = jnp.where(inside, cell + apply(residual), 0.0)
+            around = cell + old[at + t + 1]
+            free[t] = source_plane(m0 + t) - 27.0 * cell + box(around + base[0] if t == 0 else around)
+        free[0] = old[at] + apply(free[0])
+
+        @pl.when(window == 0)
+        def _():
+            pltpu.make_async_copy(t_recv, t_recv, t_rsem).wait()
+            item = unpacked(t_recv, 0)
+            for r in range(16):
+                coef[2 + r] = item(r)
+            item = unpacked(t_recv, 1)
+            for r in range(NZ):
+                e_old[r] = item(r)
+
+        arrived = e_recv.at[window]
+        pltpu.make_async_copy(arrived, arrived, e_rsem.at[window]).wait()
+        item = unpacked(arrived)
+
+        @pl.when(window == 0)
+        def _():
+            for r in range(2):
+                coef[r] = item(r)
+
+        @pl.when(jnp.logical_and(window > 0, window <= 4))
+        def _():
+            for t in range(STEPS):
+                e_old[2 * NZ - jnp.maximum(t0 - STEPS + t, 0)] = item(t)
+
+        before = jnp.where(opening, 0.0, item(STEPS - 1))
+        gives = []
+        now = None
+        for t in range(STEPS):
+            total = before + (e_old[at + t] + e_old[at + t + 1])
+            reach = max(0, STEPS - 2 - t)
+            low, high = jnp.broadcast_to(total[7:], (8, 128)), jnp.broadcast_to(total[:1], (8, 128))
+            from_low = {c: roll(low, SPAN - c) for c in range(-reach - 1, reach + 2)}
+            from_high = {c: roll(high, -SPAN - c) for c in range(-reach - 1, reach + 2)}
+            give = {}
+            for d in range(-reach, reach + 1):
+                give[0, d] = jnp.where(group8 > 0, from_low[d - 1] + from_low[d] + from_low[d + 1], 0.0)
+                give[1, d] = jnp.where(group8 < gy - 1, from_high[d - 1] + from_high[d] + from_high[d + 1], 0.0)
+            gives.append(give)
+            if t == 0:
+                mine = [spread(jnp.where(group8 == q, give[f, 0], 0.0)) for f in range(2)]
+                change = [resp[6 + f] * mine[f][:1] for f in range(2)]
+                now = jnp.where(inside, free[0] + (change[0] + change[1]), 0.0)
+            else:
+                mine = (
+                    jnp.where(top8, pltpu.roll(give[0, 0], lax.rem(128 - SPAN * q, 128), 1), 0.0),
+                    jnp.where(bottom8, pltpu.roll(give[1, 0], SPAN * (3 - q), 1), 0.0),
+                )
+                residual = free[t] + box(now)
+                residual = jnp.concatenate(
+                    [residual[:8] + mine[0], residual[8 : SPAN - 8], residual[SPAN - 8 :] + mine[1]], axis=0
+                )
+                now = jnp.where(inside, old[at + t] + apply(residual), 0.0)
             fresh[t0 + t] = now
-
-            @pl.when(backward == 0)
-            def _():
-                old[2 * NZ - jnp.minimum(t0 + t, NZ - 1)] = now
-
-            return now
-
-        lax.fori_loop(0, STEPS, true_step, base[0])
+            if t < STEPS - 1:
+                value = item(STEPS + t)
+                for s in range(t + 1):
+                    lag = t - s
+                    for f in range(2):
+                        for d in range(-lag, lag + 1):
+                            r = (0, 2, 8)[lag] + f * (2 * lag + 1) + d + lag
+                            value = value + coef[r] * gives[s][f, d]
+                before = jnp.where(inside8, value, 0.0)
+
+        @pl.when(backward == 0)
+        def _():
+            for t in range(STEPS):
+                old[2 * NZ - jnp.minimum(t0 + t, NZ - 1)] = fresh[t0 + t]
 
         @pl.when(window < 7)
         def _():
@@ -539,21 +543,21 @@
         return pl.pallas_call(
             functools.partial(kernel, n, gx, gy, depth),
             out_shape=jax.ShapeDtypeStruct(initial_field.shape, F32),
-            in_specs=[pl.BlockSpec(memory_space=pl.ANY)] * 3,
+            in_specs=[pl.BlockSpec(memory_space=pltpu.HBM)] * 3,
             out_specs=pl.BlockSpec(memory_space=pltpu.VMEM),
             scratch_shapes=[
                 vmem(NZ, SPAN, 128), vmem(NZ, SPAN, 128), vmem(SPAN * 128, 128), vmem(SPAN, 128, 128),
                 vmem(2 * NZ + 2, SPAN, 128), vmem(NZ, SPAN, 128), vmem(2 * NZ, SPAN, 128),
                 vmem(8, 2, STEPS, SPAN, 128), vmem(STEPS, SPAN, 128),
-                vmem(2 * NZ, 128), vmem(8, 16, 128), vmem(8, 3, gy, 16, 128), vmem(72, 128), vmem(3, gy, 72, 128),
-                vmem(2 * NZ + 2, 8, 128), vmem(40, 128), vmem(STEPS, 8, 128), vmem(2, SPAN, 128),
-                vmem(6, SPAN, 128), vmem(6, SPAN, 128), vmem(NZ, OWN, 128),
+                vmem(STEPS, SPAN, 128), vmem(8, 8, 128), vmem(8, 3, gy, 8, 128), vmem(2, 8, 128), vmem(3, gy, 2, 8, 128),
+                vmem(2 * NZ + 2, 8, 128), vmem(18, 8, 128), vmem(2, SPAN, 128),
+                vmem(6, SPAN, 128), vmem(8, SPAN, 128), vmem(NZ, OWN, 128),
                 dma((2, n + 2)), dma((2,)), dma((3,)), dma((2,)),
                 dma((8, 3 * gy)), dma((8,)), dma((3 * gy,)), dma,
                 dma((8, 2)), dma((8, 2)), dma((NZ,)), dma,
             ],
             compiler_params=pltpu.CompilerParams(
-                collective_id=0, has_side_effects=True, vmem_limit_bytes=40 * 1024 * 1024
+                collective_id=0, has_side_effects=True, vmem_limit_bytes=60 * 1024 * 1024
             ),
         )(initial_field, source_term, block_inverse.reshape(local * width, width))
 

time: 121 us -> 98.4 us (0.81)
  Pallas kernels: 115 us -> 96.7 us
  local copies, waits for them, and re-layouts: 5.85 us -> 1.57 us
    pallas_call x1, Pallas kernels: 115 us -> 96.7 us  [body(): pl.pallas_call(functools.partial(kernel, n, gx, gy, depth), out_shape=jax...]
    unnamed x7 -> x1, local copies, waits for them, and re-layouts: 5.85 us -> 1.57 us
where the time goes in v2:
time: 98.4 us; the launch traced here: 98.3 us
  Pallas kernels  96.7 us (98%)
  local copies, waits for them, and re-layouts  1.57 us (2%)
    pallas_call x1, Pallas kernels, body(): pl.pallas_call(functools.partial(kernel, n, gx, gy, depth), out_shape=jax...  96.7 us

profile of v2, /device:TPU:1, one launch (start us, length us, event | category | flops | bytes accessed | tf_op | source)
XLA Modules:
  0.0 98.3 jit_solution(9936612960006507295)
XLA Ops:
  0.0 96.7 %shard_map.37 = f32[2,128,128]{2,1,0:T(8,128)} custom-call(f32[2,128,128]{2,1,0:T(8,128)} %v_in.1, f32[2,128,128]{2,1,0:T(8,128)} %s_in.1, f32[16384,128]{1,0:T(8,128)} %bitcast.1), custom_call_target="tpu_custom_call" | custom-call | tf_op jit(solution)/shard_map/pallas_call | solution.py:543
  96.7 1.6 %copy.5 = f32[2,128,128]{2,1,0:T(8,128)} copy(f32[2,128,128]{2,1,0:T(8,128)} %shard_map.37) | data formatting | bytes 262144

commit v3 on v2

--- a/solution.py
+++ b/solution.py
@@ -25,8 +25,8 @@
 def kernel(
     n, gx, gy, depth,
     v_in, s_in, b_in, out,
-    v_rows, s_rows, b_rows, blocks, old, src, fresh, halo, base,
-    free, e_send, e_recv, t_send, t_recv, e_old, coef, rows2, imp, resp, out_rows,
+    v_rows, s_rows, b_rows, blocks, old, src, fresh, halo,
+    free, res, pad, last_box, start, e_send, e_recv, t_send, t_recv, e_old, coef, rows2, imp, resp, out_rows,
     field_send, field_recv, b_recv, b_send, e_ssem, e_rsem, t_ssem, t_rsem, u_ssem, u_rsem, o_ssem, o_rsem,
 ):
     g, a, q = lax.axis_index("gz"), lax.axis_index("gx"), lax.axis_index("gy")
@@ -150,6 +150,8 @@
     ends8 = jnp.logical_and(jnp.logical_or(sub8 == 0, sub8 == 7), jnp.logical_and(xlane8 >= HALO, xlane8 < HALO + OWN))
     top8, bottom8 = jnp.logical_and(sub8 == 0, group8 == 0), jnp.logical_and(sub8 == 7, group8 == 3)
 
+    zero8 = jnp.zeros((8, 128), F32)
+
     def y_sum(cells):
         up = jnp.where(group1 == 0, 0.0, roll(cells[SPAN - 1 :], SPAN))
         down = jnp.where(group1 == 3, 0.0, roll(cells[:1], -SPAN))
@@ -158,15 +160,41 @@
     def box(cells):
         return y_sum(cells + roll(cells, 1) + roll(cells, -1))
 
+    def product(residual, slot):
+        res[slot] = residual
+        acc = blocks[0] * res[slot, :1, :]
+        for j in range(1, SPAN):
+            acc = acc + blocks[j] * res[slot, j : j + 1, :]
+        rows = [acc[SPAN * i : SPAN * (i + 1)] for i in range(4)]
+        parts = []
+        for k in range(4):
+            part = rows[-k % 4]
+            for i in range(1, 4):
+                part = jnp.where(group == i, rows[(i - k) % 4], part)
+            parts.append(part)
+        return parts
+
+    def summed(parts, shifts, at=slice(None)):
+        total = None
+        for k in range(4):
+            for shift in shifts:
+                term = roll(parts[k][at], shift - SPAN * k)
+                total = term if total is None else total + term
+        return total
+
+    def plain(parts, at=slice(None)):
+        return summed(parts, (0,), at)
+
     def apply(residual):
-        acc = blocks[0] * residual[:1]
-        for j in range(1, SPAN):
-            acc = acc + blocks[j] * residual[j : j + 1]
-        a0, a1, a2, a3 = (acc[SPAN * i : SPAN * (i + 1)] for i in range(4))
-        b0 = jnp.where(low_half, a0, a2) + roll(jnp.where(low_half, a2, a0), 64)
-        b1 = jnp.where(low_half, a1, a3) + roll(jnp.where(low_half, a3, a1), 64)
-        other = jnp.where(even, b1, b0)
-        return jnp.where(even, b0 + roll(other, -SPAN), b1 + roll(other, SPAN))
+        return plain(product(residual, 7))
+
+    def boxed(parts, slot):
+        up = summed(parts, (SPAN - 1, SPAN, SPAN + 1), slice(SPAN - 8, SPAN))
+        down = summed(parts, (-SPAN - 1, -SPAN, -SPAN + 1), slice(0, 8))
+        pad[slot, :8, :] = jnp.where(group8 == 0, 0.0, up)
+        pad[slot, 8 : SPAN + 8, :] = summed(parts, (-1, 0, 1))
+        pad[slot, SPAN + 8 :, :] = jnp.where(group8 == 3, 0.0, down)
+        return pad[slot, 7 : SPAN + 7, :] + pad[slot, 8 : SPAN + 8, :] + pad[slot, 9 : SPAN + 9, :]
 
     def turn(x, carry):
         rows = pl.ds(pl.multiple_of(x * 128, 128), 128)
@@ -182,7 +210,7 @@
 
     def gather(j, carry):
         parts = [b_rows[pl.ds(SPAN * jg + j, SPAN, stride=128), :] for jg in range(4)]
-        blocks[j] = jnp.concatenate(parts, axis=0).T
+        blocks[j] = jnp.where(inside[:1], jnp.concatenate(parts, axis=0).T, 0.0)
         return carry
 
     lax.fori_loop(0, SPAN, gather, 0, unroll=4)
@@ -209,8 +237,7 @@
     lax.fori_loop(0, 6, respond, 0)
 
     def spread(value):
-        total = value + roll(value, 32)
-        return total + roll(total, 64)
+        return (value + roll(value, 32)) + (roll(value, 64) + roll(value, 96))
 
     def pair(values):
         return jnp.where(sub8 == 0, spread(values[0]), spread(values[1]))
@@ -235,7 +262,7 @@
         pair([jnp.where(group1 == 0, rows2[e, :1, :], 0.0) for e in range(2)]),
         pair([jnp.where(group1 == 3, rows2[e, SPAN - 1 :, :], 0.0) for e in range(2)]),
     ]
-    coef[0] = packed(first_pairs)
+    coef[0] = packed([zero8] * 4 + first_pairs)
     later_pairs = [dots(roll(cells[f], -d)) for f in range(2) for d in range(-1, 2)]
     for f in range(2):
         for d in range(-2, 3):
@@ -257,7 +284,7 @@
                 for i in range(4):
                     tile = jnp.where(group == i, roll(turned[SPAN * i : SPAN * (i + 1)], SPAN * (i - k)), tile)
                 place[4 * w + k] = jnp.where(inside, tile, 0.0)
-    zero_tile, zero8 = jnp.zeros((SPAN, 128), F32), jnp.zeros((8, 128), F32)
+    zero_tile = jnp.zeros((SPAN, 128), F32)
     old[NZ] = zero_tile
     old[2 * NZ + 1] = zero_tile
     e_old[NZ] = jnp.zeros((8, 128), F32)
@@ -364,29 +391,23 @@
         def source_plane(m):
             return src[m + backward * (NZ - 1 - 2 * m)]
 
-        @pl.when(opening)
-        def _():
-            base[0] = zero_tile
-
-        @pl.when(jnp.logical_not(opening))
-        def _():
-            base[0] = fresh[jnp.maximum(t0 - 1, 0)]
-
-        def base_step(t, before):
+        guesses = []
+        around = None
+        for t in range(STEPS - 1):
             cell = old[at + t]
-            residual = source_plane(m0 + t) - 27.0 * cell + box(cell + old[at + t + 1] + before)
-            now = jnp.where(inside, cell + apply(residual), 0.0)
-            base[t + 1] = now
-            return now
-
-        lax.fori_loop(0, STEPS - 1, base_step, base[0])
-
-        guesses = [edge_pair(base[k + 1, :8, :], base[k + 1, SPAN - 8 :, :], k) for k in range(STEPS - 1)]
+            near = cell + old[at + t + 1]
+            residual = source_plane(m0 + t) - 27.0 * cell + box(near if t == 0 else near + old[at + t - 1])
+            residual = residual + (jnp.where(opening, 0.0, last_box[...]) if t == 0 else boxed(around, t))
+            around = product(residual, t)
+            ends = (slice(0, 8), slice(SPAN - 8, SPAN))
+            guesses.append(edge_pair(*(cell[end] + plain(around, end) for end in ends), t))
         done = []
         for k in range(STEPS):
             tile = fresh.at[jnp.maximum(t0 - STEPS + k, 0)]
             done.append(edge_pair(tile[:8, :], tile[SPAN - 8 :, :], k))
-        e_send[window] = jnp.where(window == 0, coef[0], packed(done)) + packed([zero8] * 4 + guesses)
+        first = packed(guesses + [jnp.where(window == 0, 0.0, done[3])])
+        rest = packed([zero8] * 4 + [done[k] for k in range(3)])
+        e_send[window] = first + jnp.where(window == 0, coef[0], rest)
         edge_copies(e_send.at[window], e_recv.at[window], e_ssem.at[window], e_rsem.at[window], True)
 
         @pl.when(window > 0)
@@ -407,15 +428,23 @@
             for t in range(STEPS):
                 old[2 * NZ - jnp.maximum(t0 - STEPS + t, 0)] = merged(t)
 
+        @pl.when(opening)
+        def _():
+            start[...] = zero_tile
+
         @pl.when(jnp.logical_not(opening))
         def _():
-            base[0] = merged(STEPS - 1)
+            start[...] = merged(STEPS - 1)
 
         for t in range(STEPS):
             cell = old[at + t]
-            around = cell + old[at + t + 1]
-            free[t] = source_plane(m0 + t) - 27.0 * cell + box(around + base[0] if t == 0 else around)
-        free[0] = old[at] + apply(free[0])
+            near = cell + old[at + t + 1]
+            if t == 0:
+                near = near + start[...]
+            else:
+                near = near + (free[0] if t == 1 else old[at + t - 1])
+            value = source_plane(m0 + t) - 27.0 * cell + box(near)
+            free[t] = cell + plain(product(value, 3)) if t == 0 else value
 
         @pl.when(window == 0)
         def _():
@@ -434,16 +463,16 @@
         @pl.when(window == 0)
         def _():
             for r in range(2):
-                coef[r] = item(r)
+                coef[r] = item(4 + r)
 
         @pl.when(jnp.logical_and(window > 0, window <= 4))
         def _():
             for t in range(STEPS):
-                e_old[2 * NZ - jnp.maximum(t0 - STEPS + t, 0)] = item(t)
-
-        before = jnp.where(opening, 0.0, item(STEPS - 1))
+                e_old[2 * NZ - jnp.maximum(t0 - STEPS + t, 0)] = item(3 if t == 3 else 4 + t)
+
+        before = jnp.where(opening, 0.0, item(3))
         gives = []
-        now = None
+        around = None
         for t in range(STEPS):
             total = before + (e_old[at + t] + e_old[at + t + 1])
             reach = max(0, STEPS - 2 - t)
@@ -456,22 +485,30 @@
                 give[1, d] = jnp.where(group8 < gy - 1, from_high[d - 1] + from_high[d] + from_high[d + 1], 0.0)
             gives.append(give)
             if t == 0:
-                mine = [spread(jnp.where(group8 == q, give[f, 0], 0.0)) for f in range(2)]
-                change = [resp[6 + f] * mine[f][:1] for f in range(2)]
-                now = jnp.where(inside, free[0] + (change[0] + change[1]), 0.0)
+                gain = {
+                    key: spread(jnp.where(group8 == q, give[key], 0.0))[:1] for key in give if abs(key[1]) <= 1
+                }
+                now = free[0] + (resp[6] * gain[0, 0] + resp[7] * gain[1, 0])
             else:
                 mine = (
                     jnp.where(top8, pltpu.roll(give[0, 0], lax.rem(128 - SPAN * q, 128), 1), 0.0),
                     jnp.where(bottom8, pltpu.roll(give[1, 0], SPAN * (3 - q), 1), 0.0),
                 )
-                residual = free[t] + box(now)
+                if t == 1:
+                    residual = free[1]
+                    for f in range(2):
+                        for d in range(-1, 2):
+                            residual = residual + imp[3 * f + d + 1] * gain[f, d]
+                else:
+                    residual = free[t] + boxed(around, 1 + t)
                 residual = jnp.concatenate(
                     [residual[:8] + mine[0], residual[8 : SPAN - 8], residual[SPAN - 8 :] + mine[1]], axis=0
                 )
-                now = jnp.where(inside, old[at + t] + apply(residual), 0.0)
+                around = product(residual, 3 + t)
+                now = old[at + t] + plain(around)
             fresh[t0 + t] = now
             if t < STEPS - 1:
-                value = item(STEPS + t)
+                value = item(t)
                 for s in range(t + 1):
                     lag = t - s
                     for f in range(2):
@@ -479,6 +516,8 @@
                             r = (0, 2, 8)[lag] + f * (2 * lag + 1) + d + lag
                             value = value + coef[r] * gives[s][f, d]
                 before = jnp.where(inside8, value, 0.0)
+
+        last_box[...] = box(old[at + STEPS - 1]) + boxed(around, 4)
 
         @pl.when(backward == 0)
         def _():
@@ -548,8 +587,9 @@
             scratch_shapes=[
                 vmem(NZ, SPAN, 128), vmem(NZ, SPAN, 128), vmem(SPAN * 128, 128), vmem(SPAN, 128, 128),
                 vmem(2 * NZ + 2, SPAN, 128), vmem(NZ, SPAN, 128), vmem(2 * NZ, SPAN, 128),
-                vmem(8, 2, STEPS, SPAN, 128), vmem(STEPS, SPAN, 128),
-                vmem(STEPS, SPAN, 128), vmem(8, 8, 128), vmem(8, 3, gy, 8, 128), vmem(2, 8, 128), vmem(3, gy, 2, 8, 128),
+                vmem(8, 2, STEPS, SPAN, 128),
+                vmem(STEPS, SPAN, 128), vmem(8, SPAN, 128), vmem(8, SPAN + 16, 128), vmem(SPAN, 128), vmem(SPAN, 128),
+                vmem(8, 8, 128), vmem(8, 3, gy, 8, 128), vmem(2, 8, 128), vmem(3, gy, 2, 8, 128),
                 vmem(2 * NZ + 2, 8, 128), vmem(18, 8, 128), vmem(2, SPAN, 128),
                 vmem(6, SPAN, 128), vmem(8, SPAN, 128), vmem(NZ, OWN, 128),
                 dma((2, n + 2)), dma((2,)), dma((3,)), dma((2,)),

time: 98.4 us -> 94.4 us (0.959)
  Pallas kernels: 96.7 us -> 92.8 us
    pallas_call x1, Pallas kernels: 96.7 us -> 92.8 us  [body(): pl.pallas_call(functools.partial(kernel, n, gx, gy, depth), out_shape=jax...]
where the time goes in v3:
time: 94.4 us; the launch traced here: 94.3 us
  Pallas kernels  92.8 us (98%)
  local copies, waits for them, and re-layouts  1.57 us (2%)
    pallas_call x1, Pallas kernels, body(): pl.pallas_call(functools.partial(kernel, n, gx, gy, depth), out_shape=jax...  92.8 us

profile of v3, /device:TPU:1, one launch (start us, length us, event | category | flops | bytes accessed | tf_op | source)
XLA Modules:
  0.0 94.3 jit_solution(17120664839985696214)
XLA Ops:
  0.0 92.8 %shard_map.37 = f32[2,128,128]{2,1,0:T(8,128)} custom-call(f32[2,128,128]{2,1,0:T(8,128)} %v_in.1, f32[2,128,128]{2,1,0:T(8,128)} %s_in.1, f32[16384,128]{1,0:T(8,128)} %bitcast.1), custom_call_target="tpu_custom_call" | custom-call | tf_op jit(solution)/shard_map/pallas_call | solution.py:582
  92.8 1.6 %copy.5 = f32[2,128,128]{2,1,0:T(8,128)} copy(f32[2,128,128]{2,1,0:T(8,128)} %shard_map.37) | data formatting | bytes 262144

commit v4 on v3

--- a/solution.py
+++ b/solution.py
@@ -26,7 +26,7 @@
     n, gx, gy, depth,
     v_in, s_in, b_in, out,
     v_rows, s_rows, b_rows, blocks, old, src, fresh, halo,
-    free, res, pad, last_box, start, e_send, e_recv, t_send, t_recv, e_old, coef, rows2, imp, resp, out_rows,
+    free, res, pad, last_box, start, e_send, e_recv, t_send, t_recv, e_old, coef, rows2, imp, raw, wide, resp, out_rows,
     field_send, field_recv, b_recv, b_send, e_ssem, e_rsem, t_ssem, t_rsem, u_ssem, u_rsem, o_ssem, o_rsem,
 ):
     g, a, q = lax.axis_index("gz"), lax.axis_index("gx"), lax.axis_index("gy")
@@ -231,7 +231,8 @@
             imp[3 * e + d] = roll(cells[e], -(d - 1))
 
     def respond(i, carry):
-        resp[i] = y_sum(jnp.where(inside, apply(imp[i]), 0.0))
+        raw[i] = apply(imp[i])
+        resp[i] = y_sum(raw[i])
         return carry
 
     lax.fori_loop(0, 6, respond, 0)
@@ -272,6 +273,7 @@
                 if abs(far) <= 1:
                     term = roll(resp[3 * f + far + 1], -near)
                     total = term if total is None else total + term
+            wide[5 * f + d + 2] = total
             later_pairs.append(dots(total))
     t_send[0] = packed(later_pairs)
 
@@ -292,8 +294,9 @@
     t_send[1] = packed([edge_pair(old[z, :8, :], old[z, SPAN - 8 :, :], z % 4) for z in range(NZ)])
 
     def edge_copies(source, target, send, recv, start):
-        for x, place in enumerate(places):
-            for k in range(gy):
+        for k in sorted(range(gy), key=lambda k: -min(k, gy - k)):
+            for x in (0, 2, 1):
+                place = places[x]
                 if x == 1 and k == 0:
                     if start:
                         pltpu.make_async_copy(source, target.at[1, q], recv).start()
@@ -398,9 +401,12 @@
             near = cell + old[at + t + 1]
             residual = source_plane(m0 + t) - 27.0 * cell + box(near if t == 0 else near + old[at + t - 1])
             residual = residual + (jnp.where(opening, 0.0, last_box[...]) if t == 0 else boxed(around, t))
-            around = product(residual, t)
             ends = (slice(0, 8), slice(SPAN - 8, SPAN))
-            guesses.append(edge_pair(*(cell[end] + plain(around, end) for end in ends), t))
+            if t < STEPS - 2:
+                around = product(residual, t)
+                guesses.append(edge_pair(*(cell[end] + plain(around, end) for end in ends), t))
+            else:
+                guesses.append(edge_pair(*(cell[end] for end in ends), t) + dots(residual))
         done = []
         for k in range(STEPS):
             tile = fresh.at[jnp.maximum(t0 - STEPS + k, 0)]
@@ -438,13 +444,9 @@
 
         for t in range(STEPS):
             cell = old[at + t]
-            near = cell + old[at + t + 1]
-            if t == 0:
-                near = near + start[...]
-            else:
-                near = near + (free[0] if t == 1 else old[at + t - 1])
-            value = source_plane(m0 + t) - 27.0 * cell + box(near)
-            free[t] = cell + plain(product(value, 3)) if t == 0 else value
+            before = start[...] if t == 0 else free[t - 1] if t < 3 else old[at + t - 1]
+            value = source_plane(m0 + t) - 27.0 * cell + box(cell + old[at + t + 1] + before)
+            free[t] = cell + plain(product(value, 2 + t)) if t < 2 else value
 
         @pl.when(window == 0)
         def _():
@@ -471,7 +473,7 @@
                 e_old[2 * NZ - jnp.maximum(t0 - STEPS + t, 0)] = item(3 if t == 3 else 4 + t)
 
         before = jnp.where(opening, 0.0, item(3))
-        gives = []
+        gives, gains = [], []
         around = None
         for t in range(STEPS):
             total = before + (e_old[at + t] + e_old[at + t + 1])
@@ -484,27 +486,33 @@
                 give[0, d] = jnp.where(group8 > 0, from_low[d - 1] + from_low[d] + from_low[d + 1], 0.0)
                 give[1, d] = jnp.where(group8 < gy - 1, from_high[d - 1] + from_high[d] + from_high[d + 1], 0.0)
             gives.append(give)
-            if t == 0:
-                gain = {
-                    key: spread(jnp.where(group8 == q, give[key], 0.0))[:1] for key in give if abs(key[1]) <= 1
-                }
-                now = free[0] + (resp[6] * gain[0, 0] + resp[7] * gain[1, 0])
+            if t < 2:
+                gains.append({
+                    key: jnp.concatenate([spread(jnp.where(group8 == q, give[key], 0.0))] * 4, axis=0) for key in give
+                })
+                now = free[t] + (resp[6] * gains[t][0, 0] + resp[7] * gains[t][1, 0])
+                if t == 1:
+                    for f in range(2):
+                        for d in range(-1, 2):
+                            now = now + raw[3 * f + d + 1] * gains[0][f, d]
             else:
                 mine = (
                     jnp.where(top8, pltpu.roll(give[0, 0], lax.rem(128 - SPAN * q, 128), 1), 0.0),
                     jnp.where(bottom8, pltpu.roll(give[1, 0], SPAN * (3 - q), 1), 0.0),
                 )
-                if t == 1:
-                    residual = free[1]
+                if t == 2:
+                    residual = free[2]
                     for f in range(2):
                         for d in range(-1, 2):
-                            residual = residual + imp[3 * f + d + 1] * gain[f, d]
+                            residual = residual + imp[3 * f + d + 1] * gains[1][f, d]
+                        for d in range(-2, 3):
+                            residual = residual + wide[5 * f + d + 2] * gains[0][f, d]
                 else:
                     residual = free[t] + boxed(around, 1 + t)
                 residual = jnp.concatenate(
                     [residual[:8] + mine[0], residual[8 : SPAN - 8], residual[SPAN - 8 :] + mine[1]], axis=0
                 )
-                around = product(residual, 3 + t)
+                around = product(residual, 2 + t)
                 now = old[at + t] + plain(around)
             fresh[t0 + t] = now
             if t < STEPS - 1:
@@ -591,7 +599,7 @@
                 vmem(STEPS, SPAN, 128), vmem(8, SPAN, 128), vmem(8, SPAN + 16, 128), vmem(SPAN, 128), vmem(SPAN, 128),
                 vmem(8, 8, 128), vmem(8, 3, gy, 8, 128), vmem(2, 8, 128), vmem(3, gy, 2, 8, 128),
                 vmem(2 * NZ + 2, 8, 128), vmem(18, 8, 128), vmem(2, SPAN, 128),
-                vmem(6, SPAN, 128), vmem(8, SPAN, 128), vmem(NZ, OWN, 128),
+                vmem(6, SPAN, 128), vmem(6, SPAN, 128), vmem(10, SPAN, 128), vmem(8, SPAN, 128), vmem(NZ, OWN, 128),
                 dma((2, n + 2)), dma((2,)), dma((3,)), dma((2,)),
                 dma((8, 3 * gy)), dma((8,)), dma((3 * gy,)), dma,
                 dma((8, 2)), dma((8, 2)), dma((NZ,)), dma,

time: 94.4 us -> 91 us (0.964)
  Pallas kernels: 92.8 us -> 89.3 us
    pallas_call x1, Pallas kernels: 92.8 us -> 89.3 us  [body(): pl.pallas_call(functools.partial(kernel, n, gx, gy, depth), out_shape=jax...]
where the time goes in v4:
time: 91 us; the launch traced here: 90.9 us
  Pallas kernels  89.3 us (98%)
  local copies, waits for them, and re-layouts  1.57 us (2%)
    pallas_call x1, Pallas kernels, body(): pl.pallas_call(functools.partial(kernel, n, gx, gy, depth), out_shape=jax...  89.3 us

profile of v4, /device:TPU:1, one launch (start us, length us, event | category | flops | bytes accessed | tf_op | source)
XLA Modules:
  0.0 90.9 jit_solution(387935354316635702)
XLA Ops:
  0.0 89.3 %shard_map.37 = f32[2,128,128]{2,1,0:T(8,128)} custom-call(f32[2,128,128]{2,1,0:T(8,128)} %v_in.1, f32[2,128,128]{2,1,0:T(8,128)} %s_in.1, f32[16384,128]{1,0:T(8,128)} %bitcast.1), custom_call_target="tpu_custom_call" | custom-call | tf_op jit(solution)/shard_map/pallas_call | solution.py:590
  89.3 1.6 %copy.5 = f32[2,128,128]{2,1,0:T(8,128)} copy(f32[2,128,128]{2,1,0:T(8,128)} %shard_map.37) | data formatting | bytes 262144

commit v5 on v4

--- a/solution.py
+++ b/solution.py
@@ -147,7 +147,7 @@
     low_half, even = group < 2, group % 2 == 0
     group1 = group[:1]
     group8, xlane8, inside8, sub8 = group[:8], xlane[:8], inside[:8], row[:8]
-    ends8 = jnp.logical_and(jnp.logical_or(sub8 == 0, sub8 == 7), jnp.logical_and(xlane8 >= HALO, xlane8 < HALO + OWN))
+    ends8 = jnp.logical_and(sub8 < 2, jnp.logical_and(xlane8 >= HALO, xlane8 < HALO + OWN))
     top8, bottom8 = jnp.logical_and(sub8 == 0, group8 == 0), jnp.logical_and(sub8 == 7, group8 == 3)
 
     zero8 = jnp.zeros((8, 128), F32)
@@ -257,7 +257,7 @@
         return tile
 
     def edge_pair(top, bottom, k):
-        return jnp.where(sub8 == 0, roll(top, SPAN * k), roll(bottom, SPAN * (k - 3)))
+        return jnp.where(sub8 == 0, roll(top, SPAN * k), roll(roll(bottom, 2, 0), SPAN * (k - 3)))
 
     first_pairs = [
         pair([jnp.where(group1 == 0, rows2[e, :1, :], 0.0) for e in range(2)]),
@@ -384,6 +384,21 @@
             def _():
                 pltpu.make_async_copy(source, target, o_rsem).start()
 
+    def deliver(window):
+        at = STEPS * window
+        tiles = [fresh[at + k] for k in range(4)]
+        parts = []
+        for i in range(4):
+            part = roll(tiles[0], -SPAN * i)
+            for k in range(1, 4):
+                part = jnp.where(group == k, roll(tiles[k], SPAN * (k - i)), part)
+            parts.append(part)
+        lines = jnp.concatenate(parts, axis=0).T
+        for k in range(4):
+            z = 2 * NZ - 1 - at - k
+            out_rows[z] = lines[SPAN * k + HALO : SPAN * k + HALO + OWN]
+            out_copy(z, True)
+
     def window_step(window, carry):
         backward = window // 4
         m0 = STEPS * (window - 4 * backward)
@@ -404,7 +419,11 @@
             ends = (slice(0, 8), slice(SPAN - 8, SPAN))
             if t < STEPS - 2:
                 around = product(residual, t)
-                guesses.append(edge_pair(*(cell[end] + plain(around, end) for end in ends), t))
+                change = jnp.where(
+                    sub8 == 0, summed(around, (SPAN * t,), ends[0]),
+                    roll(summed(around, (SPAN * (t - 3),), ends[1]), 2, 0),
+                )
+                guesses.append(edge_pair(*(cell[end] for end in ends), t) + change)
             else:
                 guesses.append(edge_pair(*(cell[end] for end in ends), t) + dots(residual))
         done = []
@@ -414,7 +433,11 @@
         first = packed(guesses + [jnp.where(window == 0, 0.0, done[3])])
         rest = packed([zero8] * 4 + [done[k] for k in range(3)])
         e_send[window] = first + jnp.where(window == 0, coef[0], rest)
-        edge_copies(e_send.at[window], e_recv.at[window], e_ssem.at[window], e_rsem.at[window], True)
+        edge_copies(e_send.at[window, :4], e_recv.at[window, :, :, :4], e_ssem.at[window], e_rsem.at[window], True)
+
+        @pl.when(window > 4)
+        def _():
+            deliver(window - 1)
 
         @pl.when(window > 0)
         def _():
@@ -458,27 +481,24 @@
             for r in range(NZ):
                 e_old[r] = item(r)
 
-        arrived = e_recv.at[window]
-        pltpu.make_async_copy(arrived, arrived, e_rsem.at[window]).wait()
+        arrived, landed = e_recv.at[window], e_recv.at[window, :, :, :4]
+        pltpu.make_async_copy(landed, landed, e_rsem.at[window]).wait()
         item = unpacked(arrived)
 
-        @pl.when(window == 0)
-        def _():
-            for r in range(2):
-                coef[r] = item(4 + r)
-
-        @pl.when(jnp.logical_and(window > 0, window <= 4))
-        def _():
-            for t in range(STEPS):
-                e_old[2 * NZ - jnp.maximum(t0 - STEPS + t, 0)] = item(3 if t == 3 else 4 + t)
+        for r in range(2):
+            coef[r] = jnp.where(window == 0, item(4 + r), coef[r])
+        kept = jnp.logical_and(window > 0, window <= 4)
+        for t in range(STEPS):
+            place = jnp.where(kept, 2 * NZ - (t0 - STEPS + t), 2 * NZ + 2)
+            e_old[place] = item(3 if t == 3 else 4 + t)
 
         before = jnp.where(opening, 0.0, item(3))
-        gives, gains = [], []
+        gives, gains, planes_now = [], [], []
         around = None
         for t in range(STEPS):
             total = before + (e_old[at + t] + e_old[at + t + 1])
             reach = max(0, STEPS - 2 - t)
-            low, high = jnp.broadcast_to(total[7:], (8, 128)), jnp.broadcast_to(total[:1], (8, 128))
+            low, high = jnp.broadcast_to(total[1:2], (8, 128)), jnp.broadcast_to(total[:1], (8, 128))
             from_low = {c: roll(low, SPAN - c) for c in range(-reach - 1, reach + 2)}
             from_high = {c: roll(high, -SPAN - c) for c in range(-reach - 1, reach + 2)}
             give = {}
@@ -515,6 +535,7 @@
                 around = product(residual, 2 + t)
                 now = old[at + t] + plain(around)
             fresh[t0 + t] = now
+            planes_now.append(now)
             if t < STEPS - 1:
                 value = item(t)
                 for s in range(t + 1):
@@ -527,41 +548,25 @@
 
         last_box[...] = box(old[at + STEPS - 1]) + boxed(around, 4)
 
-        @pl.when(backward == 0)
-        def _():
-            for t in range(STEPS):
-                old[2 * NZ - jnp.minimum(t0 + t, NZ - 1)] = fresh[t0 + t]
+        for t in range(STEPS):
+            old[jnp.where(backward == 0, 2 * NZ - (t0 + t), 2 * NZ + 2)] = planes_now[t]
 
         @pl.when(window < 7)
         def _():
             halo_copy(window, 0, True)
             halo_copy(window, 1, True)
 
-        @pl.when(backward == 1)
-        def _():
-            tiles = [fresh[t0 + k] for k in range(4)]
-            parts = []
-            for i in range(4):
-                part = tiles[0] if i == 0 else roll(tiles[0], -SPAN * i)
-                for k in range(1, 4):
-                    part = jnp.where(group == k, roll(tiles[k], SPAN * (k - i)), part)
-                parts.append(part)
-            lines = jnp.concatenate(parts, axis=0).T
-            for k in range(4):
-                z = jnp.maximum(2 * NZ - 1 - t0 - k, 0)
-                out_rows[z] = lines[SPAN * k + HALO : SPAN * k + HALO + OWN]
-                out_copy(z, True)
-
         return carry
 
     lax.fori_loop(0, 8, window_step, 0)
+    deliver(7)
 
     field_copies(False)
     b_remote(False)
     edge_copies(t_send, t_recv, t_ssem, t_rsem, False)
 
     def drain(window, carry):
-        edge_copies(e_send.at[window], e_recv.at[window], e_ssem.at[window], e_rsem.at[window], False)
+        edge_copies(e_send.at[window, :4], e_recv.at[window, :, :, :4], e_ssem.at[window], e_rsem.at[window], False)
 
         @pl.when(window < 7)
         def _():
@@ -594,11 +599,11 @@
             out_specs=pl.BlockSpec(memory_space=pltpu.VMEM),
             scratch_shapes=[
                 vmem(NZ, SPAN, 128), vmem(NZ, SPAN, 128), vmem(SPAN * 128, 128), vmem(SPAN, 128, 128),
-                vmem(2 * NZ + 2, SPAN, 128), vmem(NZ, SPAN, 128), vmem(2 * NZ, SPAN, 128),
+                vmem(2 * NZ + 3, SPAN, 128), vmem(NZ, SPAN, 128), vmem(2 * NZ, SPAN, 128),
                 vmem(8, 2, STEPS, SPAN, 128),
                 vmem(STEPS, SPAN, 128), vmem(8, SPAN, 128), vmem(8, SPAN + 16, 128), vmem(SPAN, 128), vmem(SPAN, 128),
                 vmem(8, 8, 128), vmem(8, 3, gy, 8, 128), vmem(2, 8, 128), vmem(3, gy, 2, 8, 128),
-                vmem(2 * NZ + 2, 8, 128), vmem(18, 8, 128), vmem(2, SPAN, 128),
+                vmem(2 * NZ + 3, 8, 128), vmem(18, 8, 128), vmem(2, SPAN, 128),
                 vmem(6, SPAN, 128), vmem(6, SPAN, 128), vmem(10, SPAN, 128), vmem(8, SPAN, 128), vmem(NZ, OWN, 128),
                 dma((2, n + 2)), dma((2,)), dma((3,)), dma((2,)),
                 dma((8, 3 * gy)), dma((8,)), dma((3 * gy,)), dma,

time: 91 us -> 89.1 us (0.979)
  Pallas kernels: 89.3 us -> 87.4 us
    pallas_call x1, Pallas kernels: 89.3 us -> 87.4 us  [body(): pl.pallas_call(functools.partial(kernel, n, gx, gy, depth), out_shape=jax...]
where the time goes in v5:
time: 89.1 us; the launch traced here: 89 us
  Pallas kernels  87.4 us (98%)
  local copies, waits for them, and re-layouts  1.57 us (2%)
    pallas_call x1, Pallas kernels, body(): pl.pallas_call(functools.partial(kernel, n, gx, gy, depth), out_shape=jax...  87.4 us

profile of v5, /device:TPU:1, one launch (start us, length us, event | category | flops | bytes accessed | tf_op | source)
XLA Modules:
  0.0 89.0 jit_solution(1509271041583845009)
XLA Ops:
  0.0 87.4 %shard_map.37 = f32[2,128,128]{2,1,0:T(8,128)} custom-call(f32[2,128,128]{2,1,0:T(8,128)} %v_in.1, f32[2,128,128]{2,1,0:T(8,128)} %s_in.1, f32[16384,128]{1,0:T(8,128)} %bitcast.1), custom_call_target="tpu_custom_call" | custom-call | tf_op jit(solution)/shard_map/pallas_call | solution.py:595
  87.4 1.6 %copy.5 = f32[2,128,128]{2,1,0:T(8,128)} copy(f32[2,128,128]{2,1,0:T(8,128)} %shard_map.37) | data formatting | bytes 262144

commit v6 on v5

--- a/solution.py
+++ b/solution.py
@@ -27,7 +27,7 @@
     v_in, s_in, b_in, out,
     v_rows, s_rows, b_rows, blocks, old, src, fresh, halo,
     free, res, pad, last_box, start, e_send, e_recv, t_send, t_recv, e_old, coef, rows2, imp, raw, wide, resp, out_rows,
-    field_send, field_recv, b_recv, b_send, e_ssem, e_rsem, t_ssem, t_rsem, u_ssem, u_rsem, o_ssem, o_rsem,
+    field_send, field_recv, b_recv, b_send, e_ssem, e_rsem, t_ssem, t_rsem, u_ssem, u_rsem, o_ssem, o_rsem, met,
 ):
     g, a, q = lax.axis_index("gz"), lax.axis_index("gx"), lax.axis_index("gy")
     par = lax.rem(a, 2)
@@ -77,51 +77,53 @@
         return carry
 
     lax.fori_loop(0, 3 * n, greet, 0)
-    for place in places:
-        for k in range(1, gy):
-            pl.semaphore_signal(
-                barrier, inc=1, device_id=(place[0], place[1], lax.rem(q + k, gy)), device_id_type=MESH
-            )
-    pl.semaphore_wait(barrier, 3 * n - 1 + 3 * (gy - 1))
+    beside = [(place[0], place[1], lax.rem(q + k, gy)) for place in places for k in (1, gy - 1)]
+    for device in beside:
+        pl.semaphore_signal(barrier, inc=1, device_id=device, device_id_type=MESH)
+    pl.semaphore_wait(barrier, 3 * n - 1 + 6)
+    for device in beside:
+        pl.semaphore_signal(met, inc=1, device_id=device, device_id_type=MESH)
 
     fields = ((v_in, v_rows), (s_in, s_rows))
     planes = pl.ds(depth * g, depth)
 
-    def field_copies(start):
+    early = depth * g < STEPS
+
+    def field_copies(start, f):
+        source, place = fields[f]
+        arrival = field_recv.at[jnp.where(early, f, 2 * f)]
         for other in range(n):
             lo, hi = max(0, OWN * other - HALO), min(local, OWN * other + OWN + HALO)
             row = lo - (OWN * other - HALO)
             target = flip(other)
-            for f, (source, place) in enumerate(fields):
-                args = (source.at[:, pl.ds(lo, hi - lo), :], place.at[planes, pl.ds(row, hi - lo), :])
-
-                @pl.when(target != g)
-                def _():
-                    copy = remote(*args, field_send.at[f, other], field_recv.at[f], (target, a, q))
-                    if start:
-                        copy.start()
-                    else:
-                        copy.wait_send()
-
-                if start:
-                    @pl.when(target == g)
-                    def _():
-                        pltpu.make_async_copy(*args, field_recv.at[f]).start()
-
-        for f, (source, place) in enumerate(fields):
-            ends = (
-                (local - HALO, 0, (flip(n - 1), a_right, q), n),
-                (0, HALO + OWN, (flip(0), a_left, q), n + 1),
-            )
-            for line, row, device, sem in ends:
-                copy = remote(
-                    source.at[:, pl.ds(line, HALO), :], place.at[planes, pl.ds(row, HALO), :],
-                    field_send.at[f, sem], field_recv.at[f], device,
-                )
+            args = (source.at[:, pl.ds(lo, hi - lo), :], place.at[planes, pl.ds(row, hi - lo), :])
+
+            @pl.when(target != g)
+            def _():
+                copy = remote(*args, field_send.at[f, other], arrival, (target, a, q))
                 if start:
                     copy.start()
                 else:
                     copy.wait_send()
+
+            if start:
+                @pl.when(target == g)
+                def _():
+                    pltpu.make_async_copy(*args, arrival).start()
+
+        ends = (
+            (local - HALO, 0, (flip(n - 1), a_right, q), n),
+            (0, HALO + OWN, (flip(0), a_left, q), n + 1),
+        )
+        for line, row, device, sem in ends:
+            copy = remote(
+                source.at[:, pl.ds(line, HALO), :], place.at[planes, pl.ds(row, HALO), :],
+                field_send.at[f, sem], arrival, device,
+            )
+            if start:
+                copy.start()
+            else:
+                copy.wait_send()
 
     share = HALO // n
 
@@ -137,7 +139,12 @@
                 copy.wait_send()
 
     b_remote(True)
-    field_copies(True)
+    field_copies(True, 0)
+
+    @pl.when(early)
+    def _():
+        field_copies(True, 1)
+
 
     lane = lax.broadcasted_iota(jnp.int32, (SPAN, 128), 1)
     row = lax.broadcasted_iota(jnp.int32, (SPAN, 128), 0)
@@ -277,15 +284,23 @@
             later_pairs.append(dots(total))
     t_send[0] = packed(later_pairs)
 
-    for f, (place, rows_ref) in enumerate(((old, v_rows), (src, s_rows))):
-        pltpu.make_async_copy(rows_ref, rows_ref, field_recv.at[f]).wait()
-        for w in range(NZ // 4):
+    @pl.when(jnp.logical_not(early))
+    def _():
+        field_copies(True, 1)
+
+    def settle(place, rows_ref, parts, sem):
+        ref = rows_ref.at[4 * parts.start : 4 * parts.stop]
+        pltpu.make_async_copy(ref, ref, sem).wait()
+        for w in parts:
             turned = rows_ref[4 * w : 4 * w + 4].reshape(128, 128).T
             for k in range(4):
                 tile = jnp.zeros((SPAN, 128), F32)
                 for i in range(4):
                     tile = jnp.where(group == i, roll(turned[SPAN * i : SPAN * (i + 1)], SPAN * (i - k)), tile)
                 place[4 * w + k] = jnp.where(inside, tile, 0.0)
+
+    settle(old, v_rows, range(NZ // 4), field_recv.at[0])
+    settle(src, s_rows, range(1), field_recv.at[1])
     zero_tile = jnp.zeros((SPAN, 128), F32)
     old[NZ] = zero_tile
     old[2 * NZ + 1] = zero_tile
@@ -309,20 +324,19 @@
                 else:
                     copy.wait_send()
 
+    pl.semaphore_wait(met, 6)
     edge_copies(t_send, t_recv, t_ssem, t_rsem, True)
 
     def unpacked(ref, at=None):
-        tiles = []
-        for k in range(gy):
-            sides = [ref[x, k] if at is None else ref[x, k, at] for x in range(3)]
-            tiles.append(jnp.where(
-                xlane8 < HALO, roll(sides[0], -OWN), jnp.where(xlane8 >= HALO + OWN, roll(sides[2], OWN), sides[1])
-            ))
+        low_side, high_side = xlane8 < HALO, xlane8 >= HALO + OWN
         whole = []
         for k in range(4):
             tile = jnp.zeros((8, 128), F32)
             for b in range(gy):
-                tile = jnp.where(group8 == b, roll(tiles[b], SPAN * (b - k)), tile)
+                sides = [ref[x, b] if at is None else ref[x, b, at] for x in range(3)]
+                sides = [roll(sides[x], SPAN * (b - k) + OWN * (x - 1)) for x in range(3)]
+                side = jnp.where(low_side, sides[0], jnp.where(high_side, sides[2], sides[1]))
+                tile = jnp.where(group8 == b, side, tile)
             whole.append(jnp.where(inside8, tile, 0.0))
         return lambda i: roll(whole[i % 4], -2 * (i // 4), 0)
 
@@ -434,6 +448,10 @@
         rest = packed([zero8] * 4 + [done[k] for k in range(3)])
         e_send[window] = first + jnp.where(window == 0, coef[0], rest)
         edge_copies(e_send.at[window, :4], e_recv.at[window, :, :, :4], e_ssem.at[window], e_rsem.at[window], True)
+
+        @pl.when(window == 0)
+        def _():
+            settle(src, s_rows, range(1, NZ // 4), field_recv.at[2])
 
         @pl.when(window > 4)
         def _():
@@ -561,7 +579,8 @@
     lax.fori_loop(0, 8, window_step, 0)
     deliver(7)
 
-    field_copies(False)
+    field_copies(False, 0)
+    field_copies(False, 1)
     b_remote(False)
     edge_copies(t_send, t_recv, t_ssem, t_rsem, False)
 
@@ -605,9 +624,9 @@
                 vmem(8, 8, 128), vmem(8, 3, gy, 8, 128), vmem(2, 8, 128), vmem(3, gy, 2, 8, 128),
                 vmem(2 * NZ + 3, 8, 128), vmem(18, 8, 128), vmem(2, SPAN, 128),
                 vmem(6, SPAN, 128), vmem(6, SPAN, 128), vmem(10, SPAN, 128), vmem(8, SPAN, 128), vmem(NZ, OWN, 128),
-                dma((2, n + 2)), dma((2,)), dma((3,)), dma((2,)),
+                dma((2, n + 2)), dma((3,)), dma((3,)), dma((2,)),
                 dma((8, 3 * gy)), dma((8,)), dma((3 * gy,)), dma,
-                dma((8, 2)), dma((8, 2)), dma((NZ,)), dma,
+                dma((8, 2)), dma((8, 2)), dma((NZ,)), dma, pltpu.SemaphoreType.REGULAR,
             ],
             compiler_params=pltpu.CompilerParams(
                 collective_id=0, has_side_effects=True, vmem_limit_bytes=60 * 1024 * 1024

time: 89.1 us -> 88.3 us (level)
  no operation moved by 1% of the time
where the time goes in v6:
time: 88.3 us; the launch traced here: 88.2 us
  Pallas kernels  86.6 us (98%)
  local copies, waits for them, and re-layouts  1.57 us (2%)
    pallas_call x1, Pallas kernels, body(): pl.pallas_call(functools.partial(kernel, n, gx, gy, depth), out_shape=jax...  86.6 us

profile of v6, /device:TPU:1, one launch (start us, length us, event | category | flops | bytes accessed | tf_op | source)
XLA Modules:
  0.0 88.2 jit_solution(7169676897522962261)
XLA Ops:
  0.0 86.6 %shard_map.37 = f32[2,128,128]{2,1,0:T(8,128)} custom-call(f32[2,128,128]{2,1,0:T(8,128)} %v_in.1, f32[2,128,128]{2,1,0:T(8,128)} %s_in.1, f32[16384,128]{1,0:T(8,128)} %bitcast.1), custom_call_target="tpu_custom_call" | custom-call | tf_op jit(solution)/shard_map/pallas_call | solution.py:614
  86.7 1.6 %copy.5 = f32[2,128,128]{2,1,0:T(8,128)} copy(f32[2,128,128]{2,1,0:T(8,128)} %shard_map.37) | data formatting | bytes 262144

commit v7 on v6

--- a/solution.py
+++ b/solution.py
@@ -26,7 +26,7 @@
     n, gx, gy, depth,
     v_in, s_in, b_in, out,
     v_rows, s_rows, b_rows, blocks, old, src, fresh, halo,
-    free, res, pad, last_box, start, e_send, e_recv, t_send, t_recv, e_old, coef, rows2, imp, raw, wide, resp, out_rows,
+    free, res, pad, last_box, start, e_send, e_recv, t_send, t_recv, e_old, coef, rows2, imp, raw, raw2, resp2, wide, wide2, resp, out_rows,
     field_send, field_recv, b_recv, b_send, e_ssem, e_rsem, t_ssem, t_rsem, u_ssem, u_rsem, o_ssem, o_rsem, met,
 ):
     g, a, q = lax.axis_index("gz"), lax.axis_index("gx"), lax.axis_index("gy")
@@ -453,6 +453,21 @@
         def _():
             settle(src, s_rows, range(1, NZ // 4), field_recv.at[2])
 
+            for i in range(10):
+                value = plain(product(wide[i], i % 8))
+                raw2[i] = value
+                resp2[i] = y_sum(value)
+
+            for f in range(2):
+                for d in range(-3, 4):
+                    total = None
+                    for near in range(-1, 2):
+                        far = d - near
+                        if abs(far) <= 2:
+                            term = roll(resp2[5 * f + far + 2], -near)
+                            total = term if total is None else total + term
+                    wide2[7 * f + d + 3] = total
+
         @pl.when(window > 4)
         def _():
             deliver(window - 1)
@@ -485,9 +500,9 @@
 
         for t in range(STEPS):
             cell = old[at + t]
-            before = start[...] if t == 0 else free[t - 1] if t < 3 else old[at + t - 1]
+            before = start[...] if t == 0 else free[t - 1]
             value = source_plane(m0 + t) - 27.0 * cell + box(cell + old[at + t + 1] + before)
-            free[t] = cell + plain(product(value, 2 + t)) if t < 2 else value
+            free[t] = cell + plain(product(value, 2 + t)) if t < STEPS - 1 else value
 
         @pl.when(window == 0)
         def _():
@@ -524,33 +539,39 @@
                 give[0, d] = jnp.where(group8 > 0, from_low[d - 1] + from_low[d] + from_low[d + 1], 0.0)
                 give[1, d] = jnp.where(group8 < gy - 1, from_high[d - 1] + from_high[d] + from_high[d + 1], 0.0)
             gives.append(give)
-            if t < 2:
-                gains.append({
-                    key: jnp.concatenate([spread(jnp.where(group8 == q, give[key], 0.0))] * 4, axis=0) for key in give
-                })
-                now = free[t] + (resp[6] * gains[t][0, 0] + resp[7] * gains[t][1, 0])
-                if t == 1:
+            if t < STEPS - 1:
+                wing = STEPS - 1 - t
+                gain = {}
+                for f, (edge, there) in enumerate(((low, q - 1), (high, q + 1))):
+                    mine = spread(jnp.where(group8 == there, edge, 0.0))
+                    moved = {c: roll(mine, -c) for c in range(-wing - 1, wing + 2)}
+                    for d in range(-wing, wing + 1):
+                        gain[f, d] = jnp.concatenate([moved[d - 1] + moved[d] + moved[d + 1]] * 4, axis=0)
+                gains.append(gain)
+                now = free[t]
+                for s in range(t + 1):
+                    lag = t - s
                     for f in range(2):
-                        for d in range(-1, 2):
-                            now = now + raw[3 * f + d + 1] * gains[0][f, d]
+                        for d in range(-lag, lag + 1):
+                            if lag == 0:
+                                tile = resp[6 + f]
+                            else:
+                                tile = raw[3 * f + d + 1] if lag == 1 else raw2[5 * f + d + 2]
+                            now = now + tile * gains[s][f, d]
             else:
                 mine = (
                     jnp.where(top8, pltpu.roll(give[0, 0], lax.rem(128 - SPAN * q, 128), 1), 0.0),
                     jnp.where(bottom8, pltpu.roll(give[1, 0], SPAN * (3 - q), 1), 0.0),
                 )
-                if t == 2:
-                    residual = free[2]
+                residual = free[t]
+                for s, (tiles, width) in enumerate(((wide2, 3), (wide, 2), (imp, 1))):
                     for f in range(2):
-                        for d in range(-1, 2):
-                            residual = residual + imp[3 * f + d + 1] * gains[1][f, d]
-                        for d in range(-2, 3):
-                            residual = residual + wide[5 * f + d + 2] * gains[0][f, d]
-                else:
-                    residual = free[t] + boxed(around, 1 + t)
+                        for d in range(-width, width + 1):
+                            residual = residual + tiles[(2 * width + 1) * f + d + width] * gains[s][f, d]
                 residual = jnp.concatenate(
                     [residual[:8] + mine[0], residual[8 : SPAN - 8], residual[SPAN - 8 :] + mine[1]], axis=0
                 )
-                around = product(residual, 2 + t)
+                around = product(residual, 5)
                 now = old[at + t] + plain(around)
             fresh[t0 + t] = now
             planes_now.append(now)
@@ -623,7 +644,8 @@
                 vmem(STEPS, SPAN, 128), vmem(8, SPAN, 128), vmem(8, SPAN + 16, 128), vmem(SPAN, 128), vmem(SPAN, 128),
                 vmem(8, 8, 128), vmem(8, 3, gy, 8, 128), vmem(2, 8, 128), vmem(3, gy, 2, 8, 128),
                 vmem(2 * NZ + 3, 8, 128), vmem(18, 8, 128), vmem(2, SPAN, 128),
-                vmem(6, SPAN, 128), vmem(6, SPAN, 128), vmem(10, SPAN, 128), vmem(8, SPAN, 128), vmem(NZ, OWN, 128),
+                vmem(6, SPAN, 128), vmem(6, SPAN, 128), vmem(10, SPAN, 128), vmem(10, SPAN, 128), vmem(10, SPAN, 128),
+                vmem(14, SPAN, 128), vmem(8, SPAN, 128), vmem(NZ, OWN, 128),
                 dma((2, n + 2)), dma((3,)), dma((3,)), dma((2,)),
                 dma((8, 3 * gy)), dma((8,)), dma((3 * gy,)), dma,
                 dma((8, 2)), dma((8, 2)), dma((NZ,)), dma, pltpu.SemaphoreType.REGULAR,

time: 88.3 us -> 87.3 us (0.989)
  Pallas kernels: 86.6 us -> 85.6 us
    pallas_call x1, Pallas kernels: 86.6 us -> 85.6 us  [body(): pl.pallas_call(functools.partial(kernel, n, gx, gy, depth), out_shape=jax...]
where the time goes in v7:
time: 87.3 us; the launch traced here: 87.2 us
  Pallas kernels  85.6 us (98%)
  local copies, waits for them, and re-layouts  1.57 us (2%)
    pallas_call x1, Pallas kernels, body(): pl.pallas_call(functools.partial(kernel, n, gx, gy, depth), out_shape=jax...  85.6 us

profile of v7, /device:TPU:1, one launch (start us, length us, event | category | flops | bytes accessed | tf_op | source)
XLA Modules:
  0.0 87.2 jit_solution(18046408739896915581)
XLA Ops:
  0.0 85.6 %shard_map.37 = f32[2,128,128]{2,1,0:T(8,128)} custom-call(f32[2,128,128]{2,1,0:T(8,128)} %v_in.1, f32[2,128,128]{2,1,0:T(8,128)} %s_in.1, f32[16384,128]{1,0:T(8,128)} %bitcast.1), custom_call_target="tpu_custom_call" | custom-call | tf_op jit(solution)/shard_map/pallas_call | solution.py:635
  85.6 1.6 %copy.5 = f32[2,128,128]{2,1,0:T(8,128)} copy(f32[2,128,128]{2,1,0:T(8,128)} %shard_map.37) | data formatting | bytes 262144

commit v8 on v7

--- a/solution.py
+++ b/solution.py
@@ -237,12 +237,10 @@
         for d in range(3):
             imp[3 * e + d] = roll(cells[e], -(d - 1))
 
-    def respond(i, carry):
-        raw[i] = apply(imp[i])
-        resp[i] = y_sum(raw[i])
-        return carry
-
-    lax.fori_loop(0, 6, respond, 0)
+    for i in range(6):
+        value = plain(product(imp[i], i))
+        raw[i] = value
+        resp[i] = y_sum(value)
 
     def spread(value):
         return (value + roll(value, 32)) + (roll(value, 64) + roll(value, 96))

time: 87.3 us -> 86.1 us (0.986)
  Pallas kernels: 85.6 us -> 84.4 us
    pallas_call x1, Pallas kernels: 85.6 us -> 84.4 us  [body(): pl.pallas_call(functools.partial(kernel, n, gx, gy, depth), out_shape=jax...]
where the time goes in v8:
time: 86.1 us; the launch traced here: 86 us
  Pallas kernels  84.4 us (98%)
  local copies, waits for them, and re-layouts  1.57 us (2%)
    pallas_call x1, Pallas kernels, body(): pl.pallas_call(functools.partial(kernel, n, gx, gy, depth), out_shape=jax...  84.4 us

profile of v8, /device:TPU:1, one launch (start us, length us, event | category | flops | bytes accessed | tf_op | source)
XLA Modules:
  0.0 86.0 jit_solution(11321039396719812915)
XLA Ops:
  0.0 84.4 %shard_map.37 = f32[2,128,128]{2,1,0:T(8,128)} custom-call(f32[2,128,128]{2,1,0:T(8,128)} %v_in.1, f32[2,128,128]{2,1,0:T(8,128)} %s_in.1, f32[16384,128]{1,0:T(8,128)} %bitcast.1), custom_call_target="tpu_custom_call" | custom-call | tf_op jit(solution)/shard_map/pallas_call | solution.py:633
  84.4 1.6 %copy.5 = f32[2,128,128]{2,1,0:T(8,128)} copy(f32[2,128,128]{2,1,0:T(8,128)} %shard_map.37) | data formatting | bytes 262144
